TPU v7x, 256 devices: a whole 4x4x8 slice. The times are simulated.
256 devices in a mesh: grp: 16 (over y, x), sub: 16 (over z, core).
Axes of the slice: x: 4, y: 4, z: 8, core: 2. Of those that a mesh axis runs over, the one named last changes fastest.
Arguments:
- loads: bfloat16 [512, 1024, 128], P(('grp', 'sub')), may hold values from -6 to 6
- schur: bfloat16 [512, 1024, 1024], P(('grp', 'sub')), may hold values from -0.5 to 3.5, as said below
- neumann: bfloat16 [512, 1024, 1024], P(('grp', 'sub')), may hold values from -0.5 to 1.5, as said below
- basis: bfloat16 [512, 24, 1024], P(('grp', 'sub')), may hold values from -0.375 to 0.375
- dof_order: int32 [512, 4, 256], P(('grp', 'sub')), may hold values from 0 to 255, each once within a row
- primal_map: int32 [512, 24], P(('grp', 'sub')), may hold values from 0 to 2047
- emitter_counts: int32 [512], replicated, may hold values from 0 to 15
- coarse_inverse: float32 [2048, 2048], P('sub'), may hold values from -0.5 to 0.5, as said below
Outputs:
- solution: float32 [512, 1024, 128], P(('grp', 'sub'))
Inputs may be any that keep to these rules, and one draw needn't show every extreme that they name: `schur`: each block is symmetric positive definite. `neumann`: each block is symmetric positive definite. `coarse_inverse`: symmetric positive definite.
All inputs are finite; a program needn't handle non-finite values.
Results may differ from a plain program's by a relative error of at most 0.0022.
Values sent between devices are 32-bit elements; how exact they have to be, the bound alone decides.
No kernel may reach another device: no remote copies, remote signals or barrier semaphores. Data moves between devices by JAX's collectives and lax.ppermute only.
A program may use at most 64 MiB of HBM per device.

v0:
```python
import functools

import jax
import jax.numpy as jnp
from jax import lax
from jax.experimental import pallas as pl
from jax.experimental.pallas import tpu as pltpu
from jax.sharding import PartitionSpec as P

F32 = jnp.float32
BF16 = jnp.bfloat16
AXES = ("grp", "sub")
LANES = 128
TILE = 8
FACE = 256
HI = 16
COLS = 4
GATHER = HI * COLS + TILE
SLOT = 32
SUMS = 24
ACROSS = 8
VMEM_LIMIT = 40 * 1024 * 1024

NN = (((1,), (0,)), ((), ()))
NT = (((1,), (1,)), ((), ()))
TN = (((0,), (0,)), ((), ()))


def dot(left, right, dims=NN):
    return lax.dot_general(left, right, dims, preferred_element_type=F32)


def split(value):
    high = value.astype(BF16)
    return high, (value - high.astype(F32)).astype(BF16)


def wide(value):
    return jnp.concatenate(split(value), axis=1)


def fold(value):
    return value[:, :LANES] + value[:, LANES:]


def to_canon(order, value):
    return fold(dot(order, wide(value), TN))


def to_local(order, value):
    return fold(dot(order, wide(value)))


def rows(face):
    return pl.ds(pl.multiple_of(face * FACE, FACE), FACE)


class Near:
    def __init__(self, shape, dtype=F32):
        self.shape, self.dtype = tuple(shape), dtype


class Far(Near):
    pass


class Fetched:
    def __init__(self, source, scratch, done):
        self.scratch = scratch
        parts = done.shape[0]
        if parts == 1:
            self.copies = [pltpu.make_async_copy(source, scratch, done.at[0])]
        else:
            self.copies = [
                pltpu.make_async_copy(source.at[i], scratch.at[i], done.at[i])
                for i in range(parts)
            ]
        self.waiting = set(range(parts))
        self.shape = source.shape
        for copy in self.copies:
            copy.start()

    def wait(self, parts):
        for i in sorted(self.waiting & set(parts)):
            self.copies[i].wait()
        self.waiting -= set(parts)

    def __getitem__(self, at):
        first = at[0] if isinstance(at, tuple) else at
        every = range(len(self.copies))
        one = isinstance(first, int) and len(self.copies) > 1
        self.wait([first] if one else every)
        return self.scratch[at]


def send(result, part=None):
    if isinstance(result, Stored):
        result.send(part)


class Stored:
    def __init__(self, target, scratch, done):
        self.scratch, self.shape = scratch, scratch.shape
        parts = done.shape[0]
        if parts == 1:
            self.copies = [pltpu.make_async_copy(scratch, target, done.at[0])]
        else:
            self.copies = [
                pltpu.make_async_copy(scratch.at[i], target.at[i], done.at[i])
                for i in range(parts)
            ]
        self.left = list(range(parts))

    def __setitem__(self, at, value):
        self.scratch[at] = value

    def __getitem__(self, at):
        return self.scratch[at]

    def send(self, part=None):
        for i in list(self.left) if part is None else [part]:
            self.copies[i].start()
            self.left.remove(i)

    def wait(self):
        for copy in self.copies:
            copy.wait()


def parts_of(array):
    return 2 if len(array.shape) == 3 and array.shape[0] == 2 else 1


def call(kernel, outs, *args, far=(), smem=(), loose=(), scratch=()):
    n_in, n_out = len(args), len(outs)
    far_in = list(far)
    far_out = [i for i, out in enumerate(outs) if isinstance(out, Far)]
    extra = []
    for i in far_in:
        kind = pltpu.SMEM if i in smem else pltpu.VMEM
        extra.append(kind(args[i].shape, args[i].dtype))
        extra.append(pltpu.SemaphoreType.DMA((parts_of(args[i]),)))
    for i in far_out:
        extra.append(pltpu.VMEM(outs[i].shape, outs[i].dtype))
        extra.append(pltpu.SemaphoreType.DMA((parts_of(outs[i]),)))

    def whole(*refs):
        ins, results = list(refs[:n_in]), list(refs[n_in : n_in + n_out])
        rest = refs[n_in + n_out :]
        own, rest = rest[: len(scratch)], rest[len(scratch) :]
        for k, i in enumerate(far_in):
            ins[i] = Fetched(ins[i], rest[2 * k], rest[2 * k + 1])
        rest = rest[2 * len(far_in) :]
        for k, i in enumerate(far_out):
            results[i] = Stored(results[i], rest[2 * k], rest[2 * k + 1])
        kernel(*ins, *results, *own)
        for i in far_in:
            ins[i].wait(range(len(ins[i].copies)))
        for i in far_out:
            results[i].send()
        for i in far_out:
            results[i].wait()

    operands = [
        pltpu.with_memory_space_constraint(a, pltpu.HBM) if i in far and i not in loose else a
        for i, a in enumerate(args)
    ]
    return pl.pallas_call(
        whole,
        out_shape=[
            pltpu.HBM(out.shape, out.dtype)
            if isinstance(out, Far)
            else jax.ShapeDtypeStruct(out.shape, out.dtype)
            for out in outs
        ],
        in_specs=[
            pl.BlockSpec(memory_space=pl.ANY if i in far else pltpu.VMEM)
            for i in range(n_in)
        ],
        out_specs=[
            pl.BlockSpec(memory_space=pl.ANY if i in far_out else pltpu.VMEM)
            for i in range(n_out)
        ],
        scratch_shapes=list(scratch) + extra,
        compiler_params=pltpu.CompilerParams(vmem_limit_bytes=VMEM_LIMIT),
    )(*operands)


def odd_slab():
    return lax.axis_index("grp") % 2


def odd_core():
    return lax.axis_index("sub") % 2


def halo_shapes(length, place):
    return [
        place((2, length, LANES)),
        place((2, length, LANES)),
        place((length, LANES)),
        place((length, LANES)),
        place((2, length, LANES)),
    ]


def put_order(order, dof):
    row = lax.broadcasted_iota(jnp.int32, (FACE, FACE), 0)
    for s in range(2):
        for f in range(4):
            order[4 * s + f] = (row == dof[s, pl.ds(f, 1), :]).astype(F32).astype(BF16)


def put_slab_faces(faces, canon, s):
    slab, other_slab = faces[:2]
    odd = odd_slab()
    other_slab[s] = canon(s, odd)
    send(other_slab, s)
    slab[s] = canon(s, 1 - odd)
    send(slab, s)


def put_core_faces(faces, canon):
    core, other_core, inside = faces[2:]
    odd = odd_core()
    other_core[...] = canon(odd, 2 + odd)
    send(other_core)
    core[...] = canon(1 - odd, 3 - odd)
    send(core)
    inside[0] = canon(0, 3)
    inside[1] = canon(1, 2)
    send(inside)


def put_faces(faces, canon):
    for s in range(2):
        put_slab_faces(faces, canon, s)
    put_core_faces(faces, canon)


def partner(recv, s, f, span):
    slab, other_slab, core, other_core, inside = recv
    if f < 2:
        here, there = slab[s, span, :], other_slab[s, span, :]
        return jnp.where(odd_slab() == f, there, here)
    if s != f - 2:
        return inside[1 - s, span, :]
    here, there = core[span, :], other_core[span, :]
    return jnp.where(odd_core() == 1 - s, here, there)


WHOLE = pl.ds(0, FACE)


def exchange(send):
    slab, other_slab, core, other_core, inside = send
    n_grp = lax.axis_size("grp")
    n_sub = lax.axis_size("sub")

    def pairs(count, first):
        steps = [(i, i + 1) for i in range(first, count - 1, 2)]
        return steps + [(j, i) for i, j in steps]

    other_core = lax.ppermute(other_core, "sub", pairs(n_sub, 1))
    other_slab = lax.ppermute(other_slab, "grp", pairs(n_grp, 1))
    slab = lax.ppermute(slab, "grp", pairs(n_grp, 0))
    core = lax.ppermute(core, "sub", pairs(n_sub, 0))
    return [slab, other_slab, core, other_core, inside]


def share_of(weights, s, f):
    return weights[pl.ds(4 * s + f, 1), :]


def across_of(weights, s, f):
    return weights[pl.ds(ACROSS + 4 * s + f, 1), :]


LONG = FACE + 2 * 24 + TILE


def prepare_kernel(
    dof, loads, own_basis, primal, counts,
    order, weights, base, basis, *faces,
):
    grp, sub = lax.axis_index("grp"), lax.axis_index("sub")
    n_grp, n_sub = lax.axis_size("grp"), lax.axis_size("sub")
    chain = 2 * n_sub
    put_order(order, dof)
    index = primal[...].astype(F32)
    pad = jnp.full((1, SLOT - SUMS), -1.0, F32)
    index = jnp.concatenate(
        [index[0:1], pad, index[1:2], pad, jnp.zeros((1, LANES - 2 * SLOT), F32)], axis=1
    )
    index = jnp.broadcast_to(index, (TILE, LANES))
    loads.wait(range(2))
    own_basis.wait(range(2))

    def canon(s, f):
        at = order[4 * s + f]
        trace = dot(own_basis.scratch[s, :, rows(f)], at)
        face = dot(at, loads.scratch[s, rows(f), :], TN)
        return jnp.concatenate([face, trace[:, :LANES], trace[:, LANES:], index], axis=0)

    put_faces(faces, canon)

    def density(g, j):
        within = (g >= 0) & (g < n_grp) & (j >= 0) & (j < chain)
        at = jnp.where(within, g * chain + j, 0)
        return jnp.where(within, counts[at].astype(F32) + 1.0, 0.0)

    counts.wait([0])
    for s in range(2):
        j = 2 * sub + s
        own = jnp.full((1, LANES), density(grp, j), F32)
        near = ((grp - 1, j), (grp + 1, j), (grp, j - 1), (grp, j + 1))
        for f, (g, k) in enumerate(near):
            beside = jnp.full((1, LANES), density(g, k), F32)
            weights[pl.ds(4 * s + f, 1), :] = own / (own + beside)
            weights[pl.ds(ACROSS + 4 * s + f, 1), :] = beside / (own + beside)
    base[...] = loads[...]
    for s in range(2):
        padded = [own_basis[s].astype(F32), jnp.zeros((SLOT - SUMS, 4 * FACE), F32)]
        basis[s] = jnp.concatenate(padded, axis=0).astype(BF16)


def settle_kernel(own, other, neumann, high, low, kept, done):
    copy = pltpu.make_async_copy(neumann, kept, done.at[0])
    copy.start()
    upper = odd_core() == 1
    for half in range(2):
        at = pl.ds(half * LANES, LANES)
        mine, theirs = own[...], other[...]
        value = jnp.where(upper, mine, theirs) if half else jnp.where(upper, theirs, mine)
        first, second = split(value)
        high[at, :] = first
        low[at, :] = second
    copy.wait()


def put_message(message, values, start):
    flat = jnp.transpose(values)
    owners = LANES // COLS
    for c in range(COLS):
        message[pl.ds(start + c, owners, stride=TILE), :] = flat[c * owners : (c + 1) * owners]


def get_message(message, start):
    owners = LANES // COLS
    flat = jnp.concatenate(
        [message[pl.ds(start + c, owners, stride=TILE), :] for c in range(COLS)], axis=0
    )
    return jnp.transpose(flat)


def residual_kernel(
    order, inside, other_core, other_slab, core, slab, weights, base, basis, neumann,
    local, traces, message, *faces,
):
    recv = (slab, other_slab, core, other_core, inside)
    moments = []
    scaled = []
    for s in range(2):
        pieces = []
        for f in range(4):
            at = order[4 * s + f]
            beside = dot(at, partner(recv, s, f, WHOLE).astype(BF16))
            value = base[s, rows(f), :].astype(F32) + beside
            pieces.append((share_of(weights, s, f) * value).astype(BF16))
            left = partner(recv, s, f, pl.ds(FACE, 24))
            right = partner(recv, s, f, pl.ds(FACE + 24, 24))
            trace = dot(jnp.concatenate([left, right], axis=1).astype(BF16), at, NT)
            both = [
                basis[s, :, rows(f)].astype(F32), trace, jnp.zeros((SLOT - SUMS, FACE), F32)
            ]
            traces[4 * s + f] = jnp.concatenate(both, axis=0).astype(BF16)
        scaled.append(jnp.concatenate(pieces, axis=0))
        moments.append(dot(basis[s], scaled[s]))
    moments.append(jnp.zeros((LANES - 2 * SLOT, LANES), F32))
    put_message(message, jnp.concatenate(moments, axis=0), 0)
    tile = pl.ds(FACE + 48, TILE)
    own = inside[0, tile, :][0:1]
    lower = partner(recv, 0, 0, tile)[0:1]
    upper = partner(recv, 0, 1, tile)[0:1]
    previous = partner(recv, 0, 2, tile)[0:1]
    following = partner(recv, 1, 3, tile)[0:1]
    first = jnp.concatenate([own[:, : 2 * SLOT], lower[:, : 2 * SLOT]], axis=1)
    second = jnp.concatenate(
        [upper[:, : 2 * SLOT], previous[:, SLOT : 2 * SLOT], following[:, :SLOT]], axis=1
    )
    owners = LANES // COLS
    for c, line in ((COLS, first), (COLS + 1, second)):
        message[pl.ds(c, owners, stride=TILE), :] = jnp.broadcast_to(line, (owners, LANES))
    for c in range(COLS + 2, TILE):
        message[pl.ds(c, owners, stride=TILE), :] = jnp.zeros((owners, LANES), F32)
    send(traces)

    def canon(s, f):
        return to_canon(order[4 * s + f], local[s, rows(f), :])

    for s in range(2):
        product = dot(neumann[s], scaled[s])
        for f in range(4):
            part = product[f * FACE : f * FACE + FACE]
            local[s, rows(f), :] = share_of(weights, s, f) * part
        send(local, s)
        put_slab_faces(faces, canon, s)
    put_core_faces(faces, canon)


def high_low(maps, row):
    at = maps[pl.ds(row, 1), :].astype(jnp.int32)
    return at >> 7, at & (LANES - 1)


def scatter(received, maps, row_at, gathered, lhs, hot, lines):
    owners = received.shape[0] // TILE
    row = lax.broadcasted_iota(jnp.int32, (LANES, LANES), 0)
    tile_row = lax.broadcasted_iota(jnp.int32, (TILE, LANES), 0)
    total = jnp.zeros((TILE, LANES), F32)
    for d in range(owners):
        block = received[pl.ds(TILE * d, TILE), :]
        total = total + block
        span = pl.ds(d * LANES, LANES)
        highs = []
        for line in range(lines):
            high, low = high_low(maps, row_at(d, line))
            highs.append(high)
            hot[pl.ds(line * LANES, LANES), span] = (row == low).astype(F32).astype(BF16)
        high = highs[0]
        if lines == 2:
            high = jnp.where(tile_row < COLS, highs[0], highs[1])
        spread = jnp.concatenate([jnp.where(high == h, block, 0.0) for h in range(HI)], axis=0)
        first, second = split(spread)
        lhs[pl.ds(0, LANES), span] = first
        lhs[pl.ds(LANES, LANES), span] = second
    both = dot(lhs[...], hot[pl.ds(0, lines * LANES), :], NT)
    both = both[:LANES] + both[LANES:]
    packed = []
    for h in range(HI):
        value = both[TILE * h : TILE * h + COLS, :LANES]
        if lines == 2:
            value = value + both[TILE * h + COLS : TILE * h + TILE, LANES:]
        packed.append(value)
    packed = jnp.concatenate(packed + [total], axis=0)
    for z in range(gathered.shape[0] // GATHER):
        gathered[pl.ds(GATHER * z, GATHER), :] = packed


def scatter_kernel(received, gathered, maps, lhs, hot):
    for d in range(received.shape[0] // TILE):
        maps[pl.ds(2 * d, 2), :] = received[pl.ds(TILE * d + COLS, 2), :]
    send(maps)
    scatter(received, received, lambda d, k: TILE * d + COLS + k, gathered, lhs, hot, 1)


def coarse_kernel(gathered, high, low, slab, scalars):
    n_z = gathered.shape[0] // GATHER
    total = gathered[pl.ds(0, GATHER), :]
    for z in range(1, n_z):
        total = total + gathered[pl.ds(GATHER * z, GATHER), :]
    scalars[...] = total[HI * COLS :]
    flat = jnp.concatenate([total[COLS * h : COLS * h + COLS] for h in range(HI)], axis=1)
    first, second = split(flat)
    both = dot(jnp.concatenate([first, second], axis=0), high[...], NT)
    result = both[:COLS] + both[COLS:] + dot(first, low[...], NT)
    tile = jnp.concatenate([result[:, :LANES], result[:, LANES:]], axis=0)
    for z in range(n_z):
        slab[pl.ds(TILE * z, TILE), :] = tile


def pick_kernel(coarse, maps, scalars, message):
    owners = maps.shape[0] // 2
    row = lax.broadcasted_iota(jnp.int32, (LANES, LANES), 0)
    tile_row = lax.broadcasted_iota(jnp.int32, (TILE, LANES), 0)
    lane = lax.broadcasted_iota(jnp.int32, (TILE, LANES), 1)
    carried = (lane >= SUMS) & (lane < SLOT) & (tile_row < COLS)
    first, second = split(coarse[...])
    table = jnp.concatenate([first, second], axis=0)
    extra = scalars[...]
    for d in range(owners):
        pair = [high_low(maps, 2 * d + line) for line in range(2)]
        hot = jnp.concatenate(
            [(row == low).astype(F32).astype(BF16) for _, low in pair], axis=1
        )
        both = dot(table, hot)
        both = both[: HI * COLS] + both[HI * COLS :]
        picked = []
        for line, (high, _) in enumerate(pair):
            value = both[:, line * LANES : line * LANES + LANES]
            total = jnp.zeros((TILE, LANES), F32)
            for v in range(HI * COLS // TILE):
                here = high == (tile_row // COLS + 2 * v)
                total = total + jnp.where(here, value[TILE * v : TILE * v + TILE], 0.0)
            picked.append(total + pltpu.roll(total, COLS, 0))
        value = jnp.where(tile_row < COLS, picked[0], picked[1])
        message[pl.ds(TILE * d, TILE), :] = jnp.where(carried, extra, value)


def slots(message):
    first, second = get_message(message, 0), get_message(message, COLS)
    return [v[SLOT * i : SLOT * i + SLOT] for v in (first, second) for i in range(4)]


def neighbour(s, f):
    if f < 2:
        return 2 + 2 * f + s
    if s == f - 2:
        return 6 + s
    return 1 - s


def spread(traces, weights, picked, s, f):
    both = jnp.concatenate(
        [share_of(weights, s, f) * picked[s], across_of(weights, s, f) * picked[neighbour(s, f)]], axis=0
    )
    return fold(dot(traces[4 * s + f], wide(both), TN))


def column_sum(value):
    return jnp.sum(value, axis=0, keepdims=True)


def direction_kernel(
    returned, dof, traces, weights, local, inside, other_core, other_slab, core, slab, loads,
    schur,
    direction, image, message, *rest,
):
    faces, order = rest[:5], rest[5]
    put_order(order, dof)
    recv = (slab, other_slab, core, other_core, inside)
    picked = slots(returned)
    sums = [jnp.zeros((SLOT, LANES), F32) for _ in range(8)]
    rz = jnp.zeros((1, LANES), F32)
    curve = jnp.zeros((1, LANES), F32)

    def canon(s, f):
        return to_canon(order[4 * s + f], image[s, rows(f), :])

    for s in range(2):
        for f in range(4):
            value = local[s, rows(f), :] + spread(traces, weights, picked, s, f)
            value = value + to_local(order[4 * s + f], partner(recv, s, f, WHOLE))
            direction[s, rows(f), :] = value
            rz = rz + column_sum(loads[s, rows(f), :].astype(F32) * value)
        whole = direction[s]
        product = dot(schur[s], whole.astype(BF16))
        image[s] = product
        curve = curve + column_sum(whole * product)
        send(direction, s)
        send(image, s)
        put_slab_faces(faces, canon, s)
    put_core_faces(faces, canon)
    for s in range(2):
        for f in range(4):
            both = fold(dot(traces[4 * s + f], wide(image[s, rows(f), :])))
            sums[s] = sums[s] + share_of(weights, s, f) * both[:SLOT]
            to = neighbour(s, f)
            sums[to] = sums[to] + across_of(weights, s, f) * both[SLOT:]
    carried = [rz, curve, jnp.zeros((SLOT - SUMS - 2, LANES), F32)]
    first = [sums[0][:SUMS]] + carried + sums[1:4]
    put_message(message, jnp.concatenate(first, axis=0), 0)
    put_message(message, jnp.concatenate(sums[4:], axis=0), COLS)


def image_kernel(
    received, maps, dof, weights, partial, inside, other_core, other_slab, core, slab, neumann,
    gathered, local, *rest,
):
    faces, (lhs, hot, order) = rest[:5], rest[5:]
    put_order(order, dof)
    recv = (slab, other_slab, core, other_core, inside)
    scatter(received, maps, lambda d, k: 2 * d + k, gathered, lhs, hot, 2)

    def canon(s, f):
        return to_canon(order[4 * s + f], local[s, rows(f), :])

    for s in range(2):
        pieces = []
        for f in range(4):
            beside = to_local(order[4 * s + f], partner(recv, s, f, WHOLE))
            value = partial[s, rows(f), :] + beside
            pieces.append(wide(share_of(weights, s, f) * value))
        product = fold(dot(neumann[s], jnp.concatenate(pieces, axis=0)))
        for f in range(4):
            part = product[f * FACE : f * FACE + FACE]
            local[s, rows(f), :] = share_of(weights, s, f) * part
        send(local, s)
        put_slab_faces(faces, canon, s)
    put_core_faces(faces, canon)


def last_kernel(
    returned, dof, traces, weights, local, inside, other_core, other_slab, core, slab, direction,
    loads, schur,
    search, scalars, message, order,
):
    put_order(order, dof)
    recv = (slab, other_slab, core, other_core, inside)
    picked = slots(returned)
    carried = picked[0][SUMS : SUMS + 2]
    rz, curve = carried[0:1], carried[1:2]
    step = rz / curve
    scalars[...] = jnp.concatenate([rz, curve, step, jnp.zeros((TILE - 3, LANES), F32)], axis=0)
    along = jnp.zeros((1, LANES), F32)
    same = jnp.zeros((1, LANES), F32)
    cross = jnp.zeros((1, LANES), F32)
    for s in range(2):
        for f in range(4):
            value = local[s, rows(f), :] + spread(traces, weights, picked, s, f)
            value = value + to_local(order[4 * s + f], partner(recv, s, f, WHOLE))
            value = direction[s, rows(f), :] - step * value
            search[s, rows(f), :] = value
            along = along + column_sum(loads[s, rows(f), :].astype(F32) * value)
        whole = search[s]
        send(search, s)
        rounded = whole.astype(BF16)
        product = dot(schur[s], rounded)
        twice = 2.0 * whole - rounded.astype(F32)
        same = same + column_sum(twice * product)
        cross = cross + column_sum(direction[s] * product)
    rz_next = along - step * cross
    tile = jnp.concatenate([rz_next, same, cross, jnp.zeros((TILE - 3, LANES), F32)], axis=0)
    for d in range(message.shape[0] // TILE):
        message[pl.ds(TILE * d, TILE), :] = tile


def sum_tiles(received):
    total = received[pl.ds(0, TILE), :]
    for d in range(1, received.shape[0] // TILE):
        total = total + received[pl.ds(TILE * d, TILE), :]
    return total


def sum_kernel(received, out):
    total = sum_tiles(received)
    for z in range(out.shape[0] // TILE):
        out[pl.ds(TILE * z, TILE), :] = total


def finish_kernel(received, scalars, direction, search, out):
    total = sum_tiles(received)
    rz, curve, step = scalars[0:1, :], scalars[1:2, :], scalars[2:3, :]
    rz_next, same, cross = total[0:1], total[1:2], total[2:3]
    beta = rz_next / rz
    curve_next = same + 2.0 * beta * cross + beta * beta * curve
    step_next = rz_next / curve_next
    along = step + step_next * beta
    for s in range(2):
        out[s] = along * direction[s] + step_next * search[s]
        send(out, s)


def settle(own, other, neumann):
    return pl.pallas_call(
        settle_body,
        out_shape=[
            jax.ShapeDtypeStruct((2 * LANES, own.shape[1]), BF16),
            jax.ShapeDtypeStruct((2 * LANES, own.shape[1]), BF16),
            jax.ShapeDtypeStruct(neumann.shape, BF16),
        ],
        in_specs=[pl.BlockSpec(memory_space=pl.ANY)] * 3,
        out_specs=[pl.BlockSpec(memory_space=pltpu.VMEM)] * 3,
        scratch_shapes=[
            pltpu.VMEM(own.shape, F32),
            pltpu.VMEM(own.shape, F32),
            pltpu.SemaphoreType.DMA((1,)),
            pltpu.SemaphoreType.DMA((1,)),
            pltpu.SemaphoreType.DMA((1,)),
        ],
        compiler_params=pltpu.CompilerParams(vmem_limit_bytes=VMEM_LIMIT),
    )(
        pltpu.with_memory_space_constraint(own, pltpu.HBM),
        other,
        pltpu.with_memory_space_constraint(neumann, pltpu.HBM),
    )


def settle_body(own, other, neumann, high, low, kept, own_here, other_here, a, b, c):
    fetched = Fetched(own, own_here, a), Fetched(other, other_here, b)
    settle_kernel(*fetched, neumann, high, low, kept, c)


def body(loads, schur, neumann, basis, dof_order, primal_map, emitter_counts, coarse_inverse):
    n_grp = lax.axis_size("grp")
    n_sub = lax.axis_size("sub")
    n_z = n_sub // 2
    vector = Far((2, 4 * FACE, LANES))
    small = Near((TILE, LANES))
    owners = 2 * n_grp
    message_shape = Near((owners * TILE, LANES))

    plane = [
        [g * n_sub + 2 * z + c for g in range(n_grp) for c in range(2)] for z in range(n_z)
    ]
    column = [
        [g * n_sub + 2 * z + c for z in range(n_z)] for g in range(n_grp) for c in range(2)
    ]

    def to_owners(value):
        return lax.all_to_all(value, AXES, 0, 0, axis_index_groups=plane, tiled=True)

    def along_z(value):
        return lax.all_to_all(value, AXES, 0, 0, axis_index_groups=column, tiled=True)

    swap = [(i, i ^ 1) for i in range(n_sub)]
    other = lax.ppermute(coarse_inverse, "sub", swap)
    order, weights, base, padded, *faces = call(
        prepare_kernel,
        [
            Near((8, FACE, FACE), BF16),
            Near((2 * TILE, LANES)),
            Near(loads.shape, BF16),
            Near((2, SLOT, 4 * FACE), BF16),
        ]
        + halo_shapes(LONG, Near),
        dof_order, loads, basis, primal_map, emitter_counts,
        far=(0, 1, 2, 3, 4), smem=(4,),
    )

    def halo(faces):
        slab, other_slab, core, other_core, inside = exchange(faces)
        return inside, other_core, other_slab, core, slab

    recv = halo(faces)
    high, low, kept = settle(coarse_inverse, other, neumann)
    one_hot = pltpu.VMEM((8, FACE, FACE), BF16)
    lists = (
        pltpu.VMEM((2 * LANES, owners * LANES), BF16),
        pltpu.VMEM((2 * LANES, owners * LANES), BF16),
    )
    gathered_shape = Near((n_z * GATHER, LANES))

    def coarse_solve(gathered, maps):
        slab, sums = call(
            coarse_kernel, [Near((n_z * TILE, LANES)), small], along_z(gathered), high, low
        )
        (picked,) = call(
            pick_kernel, [message_shape], along_z(slab), maps, sums
        )
        return to_owners(picked)

    local, traces, message, *faces = call(
        residual_kernel,
        [vector, Near((8, 2 * SLOT, FACE), BF16), message_shape] + halo_shapes(FACE, Far),
        order, *recv, weights, base, padded, kept,
    )
    recv = halo(faces)
    gathered, maps = call(
        scatter_kernel, [gathered_shape, Near((2 * owners, LANES))], to_owners(message),
        scratch=lists,
    )
    returned = coarse_solve(gathered, maps)
    direction, partial, message, *faces = call(
        direction_kernel,
        [vector, vector, message_shape] + halo_shapes(FACE, Far),
        returned, dof_order, traces, weights, local, *recv, loads, schur,
        far=[1] + list(range(4, 12)), loose=range(6, 10), scratch=(one_hot,),
    )
    recv = halo(faces)
    gathered, local, *faces = call(
        image_kernel,
        [gathered_shape, vector] + halo_shapes(FACE, Far),
        to_owners(message), maps, dof_order, weights, partial, *recv, neumann,
        far=[2] + list(range(4, 11)), loose=range(6, 10), scratch=lists + (one_hot,),
    )
    recv = halo(faces)
    returned = coarse_solve(gathered, maps)
    search, scalars, message = call(
        last_kernel,
        [vector, small, message_shape],
        returned, dof_order, traces, weights, local, *recv, direction, loads, schur,
        far=[1] + list(range(4, 13)), loose=range(6, 10), scratch=(one_hot,),
    )
    (sums,) = call(sum_kernel, [Near((n_z * TILE, LANES))], to_owners(message))
    (out,) = call(
        finish_kernel, [vector], along_z(sums), scalars, direction, search, far=(2, 3)
    )
    return out


def solution(mesh):
    in_specs = (
        P(AXES, None, None),
        P(AXES, None, None),
        P(AXES, None, None),
        P(AXES, None, None),
        P(AXES, None, None),
        P(AXES, None),
        P(),
        P("sub", None),
    )
    return jax.shard_map(
        body, mesh=mesh, in_specs=in_specs, out_specs=P(AXES, None, None), check_vma=False
    )
```

profile of v0, /device:TPU:1, one launch (start us, length us, event | category | flops | bytes accessed | tf_op | source)
XLA Modules:
  0.0 195.9 jit_solution(9232744531001333884)
XLA Ops:
  0.0 3.2 %collective-permute-start.4 = (f32[128,2048]{1,0:T(8,128)}, f32[128,2048]{1,0:T(8,128)S(1)}, u32[]{:S(2)}, u32[]{:S(2)}) collective-permute-start(f32[128,2048]{1,0:T(8,128)} %own.1), channel_id=1, source_target_pairs={{0,1},{1,0},{2,3},{3,2},{4,5},{5,4},{6,7},{7,6},{8,9},{9,8},{10,11... | collective-permute-start | bytes 3145736 | tf_op jit(solution)/shard_map/ppermute | solution.py:707
  7.7 4.0 %collective-permute-start = (f32[312,128]{1,0:T(8,128)S(1)}, f32[312,128]{1,0:T(8,128)S(1)}, u32[]{:S(2)}, u32[]{:S(2)}) collective-permute-start(f32[312,128]{1,0:T(8,128)S(1)} %get-tuple-element.51), channel_id=1, source_target_pairs={{1,2},{3,4},{5,6},{7,8},{9,10},{11,12},{13,14},{2,1},{4,3},{6,5},{... | collective-permute-start | bytes 479240 | tf_op jit(solution)/shard_map/ppermute | solution.py:264
  15.5 4.7 %shard_map.84 = (f32[2,1024,128]{2,1,0:T(8,128)}, bf16[8,64,256]{2,1,0:T(8,128)(2,1)S(1)}, f32[256,128]{1,0:T(8,128)S(1)}, f32[2,256,128]{2,1,0:T(8,128)}, f32[2...) custom-call(bf16[8,256,256]{2,1,0:T(8,128)(2,1)S(1)} %get-tuple-element.49.refs_0_, ...), custom_call_target="tpu_custom_call" | custom-call | tf_op jit(solution)/shard_map/pallas_call | solution.py:168
  20.2 16.1 %all_to_all.110 = f32[32,8,128]{2,1,0:T(8,128)S(1)} all-to-all(f32[32,8,128]{2,1,0:T(8,128)S(1)} %bitcast.32), channel_id=1, replica_groups={{0,1,16,17,32,33,48,49,64,65,80,81,96,97,112,113,128,129,144,145,160,16..., dimensions={0} | all-to-all | bytes 262144 | tf_op jit(solution)/shard_map/all_to_all | solution.py:701
  38.5 8.2 %all-to-all-start.1 = ((f32[8,72,128]{2,1,0:T(8,128)}), f32[8,72,128]{2,1,0:T(8,128)S(1)}, u32[]{:S(2)}, u32[]{:S(2)}) async-start(f32[8,72,128]{2,1,0:T(8,128)} %bitcast.2), calls=%async_computation.1 | async-start | bytes 589824 | tf_op jit(solution)/shard_map/all_to_all | solution.py:704
  49.2 9.9 %all-to-all-done.1 = f32[8,72,128]{2,1,0:T(8,128)S(1)} async-done(((f32[8,72,128]{2,1,0:T(8,128)}), f32[8,72,128]{2,1,0:T(8,128)S(1)}, u32[]{:S(2)}, u32[]{:S(2)}) %all-to-all-start.1) | async-done | bytes 294944 | tf_op jit(solution)/shard_map/all_to_all | solution.py:704
  60.4 3.3 %all-to-all-start.2 = ((f32[8,8,128]{2,1,0:T(8,128)}), f32[8,8,128]{2,1,0:T(8,128)S(1)}, u32[]{:S(2)}, u32[]{:S(2)}) async-start(f32[8,8,128]{2,1,0:T(8,128)} %bitcast.4), calls=%async_computation.2 | async-start | bytes 65536 | tf_op jit(solution)/shard_map/all_to_all | solution.py:704
  63.7 4.6 %collective-permute-start.5 = (f32[256,128]{1,0:T(8,128)}, f32[256,128]{1,0:T(8,128)S(1)}, u32[]{:S(2)}, u32[]{:S(2)}) collective-permute-start(f32[256,128]{1,0:T(8,128)} %get-tuple-element.69), channel_id=1, source_target_pairs={{1,2},{3,4},{5,6},{7,8},{9,10},{11,12},{13,14},{2,1},{4,3},{6,5},{... | collective-permute-start | bytes 393224 | tf_op jit(solution)/shard_map/ppermute | solution.py:264
  72.2 5.9 %all-to-all-start.3 = ((f32[32,8,128]{2,1,0:T(8,128)}), f32[32,8,128]{2,1,0:T(8,128)S(1)}, u32[]{:S(2)}, u32[]{:S(2)}) async-start(f32[32,8,128]{2,1,0:T(8,128)} %bitcast.6), calls=%async_computation.3 | async-start | bytes 262144 | tf_op jit(solution)/shard_map/all_to_all | solution.py:701
  78.2 7.7 %all-to-all-done.3 = f32[32,8,128]{2,1,0:T(8,128)S(1)} async-done(((f32[32,8,128]{2,1,0:T(8,128)}), f32[32,8,128]{2,1,0:T(8,128)S(1)}, u32[]{:S(2)}, u32[]{:S(2)}) %all-to-all-start.3) | async-done | bytes 131104 | tf_op jit(solution)/shard_map/all_to_all | solution.py:701
  85.9 8.8 %shard_map.88 = (f32[2,1024,128]{2,1,0:T(8,128)}, f32[2,1024,128]{2,1,0:T(8,128)}, f32[256,128]{1,0:T(8,128)S(1)}, f32[2,256,128]{2,1,0:T(8,128)}, f32[2,256,128...) custom-call(f32[256,128]{1,0:T(8,128)S(1)} %bitcast.22, s32[2,4,256]{2,1,0:T(4,128)} %refs_1_.5, ...), custom_call_target="tpu_custom_call" | custom-call | tf_op jit(solution)/shard_map/pallas_call | solution.py:168
  97.1 2.9 %collective-permute-start.9 = (f32[256,128]{1,0:T(8,128)}, f32[256,128]{1,0:T(8,128)S(1)}, u32[]{:S(2)}, u32[]{:S(2)}) collective-permute-start(f32[256,128]{1,0:T(8,128)} %get-tuple-element.76), channel_id=1, source_target_pairs={{1,2},{3,4},{5,6},{7,8},{9,10},{11,12},{13,14},{2,1},{4,3},{6,5},{... | collective-permute-start | bytes 393224 | tf_op jit(solution)/shard_map/ppermute | solution.py:264
  100.1 14.5 %all_to_all.111 = f32[32,8,128]{2,1,0:T(8,128)S(1)} all-to-all(f32[32,8,128]{2,1,0:T(8,128)S(1)} %bitcast.31), channel_id=1, replica_groups={{0,1,16,17,32,33,48,49,64,65,80,81,96,97,112,113,128,129,144,145,160,16..., dimensions={0} | all-to-all | bytes 262144 | tf_op jit(solution)/shard_map/all_to_all | solution.py:701
  114.6 9.0 %shard_map.89 = (f32[576,128]{1,0:T(8,128)}, f32[2,1024,128]{2,1,0:T(8,128)}, f32[2,256,128]{2,1,0:T(8,128)}, f32[2,256,128]{2,1,0:T(8,128)}, f32[256,128]{1,0:T...) custom-call(f32[256,128]{1,0:T(8,128)S(1)} %bitcast.24, f32[64,128]{1,0:T(8,128)S(1)} %get-tuple-element.64.refs_1_, ...), custom_call_target="tpu_custom_call" | custom-call | tf_op jit(solution)/shard_map/pallas_call | solution.py:168
  123.6 3.4 %all-to-all-start.5 = ((f32[8,72,128]{2,1,0:T(8,128)}), f32[8,72,128]{2,1,0:T(8,128)S(1)}, u32[]{:S(2)}, u32[]{:S(2)}) async-start(f32[8,72,128]{2,1,0:T(8,128)} %bitcast.10), calls=%async_computation.5 | async-start | bytes 589824 | tf_op jit(solution)/shard_map/all_to_all | solution.py:704
  129.5 10.5 %all-to-all-done.5 = f32[8,72,128]{2,1,0:T(8,128)S(1)} async-done(((f32[8,72,128]{2,1,0:T(8,128)}), f32[8,72,128]{2,1,0:T(8,128)S(1)}, u32[]{:S(2)}, u32[]{:S(2)}) %all-to-all-start.5) | async-done | bytes 294944 | tf_op jit(solution)/shard_map/all_to_all | solution.py:704
  141.3 3.3 %all-to-all-start.6 = ((f32[8,8,128]{2,1,0:T(8,128)}), f32[8,8,128]{2,1,0:T(8,128)S(1)}, u32[]{:S(2)}, u32[]{:S(2)}) async-start(f32[8,8,128]{2,1,0:T(8,128)} %bitcast.12), calls=%async_computation.6 | async-start | bytes 65536 | tf_op jit(solution)/shard_map/all_to_all | solution.py:704
  144.6 3.9 %collective-permute-start.13 = (f32[256,128]{1,0:T(8,128)}, f32[256,128]{1,0:T(8,128)S(1)}, u32[]{:S(2)}, u32[]{:S(2)}) collective-permute-start(f32[256,128]{1,0:T(8,128)} %get-tuple-element.85), channel_id=1, source_target_pairs={{1,2},{3,4},{5,6},{7,8},{9,10},{11,12},{13,14},{2,1},{4,3},{6,5},{... | collective-permute-start | bytes 393224 | tf_op jit(solution)/shard_map/ppermute | solution.py:264
  148.9 2.6 %all-to-all-done.6 = f32[8,8,128]{2,1,0:T(8,128)S(1)} async-done(((f32[8,8,128]{2,1,0:T(8,128)}), f32[8,8,128]{2,1,0:T(8,128)S(1)}, u32[]{:S(2)}, u32[]{:S(2)}) %all-to-all-start.6) | async-done | bytes 32800 | tf_op jit(solution)/shard_map/all_to_all | solution.py:704
  153.1 5.2 %all-to-all-start.7 = ((f32[32,8,128]{2,1,0:T(8,128)}), f32[32,8,128]{2,1,0:T(8,128)S(1)}, u32[]{:S(2)}, u32[]{:S(2)}) async-start(f32[32,8,128]{2,1,0:T(8,128)} %bitcast.14), calls=%async_computation.7 | async-start | bytes 262144 | tf_op jit(solution)/shard_map/all_to_all | solution.py:701
  158.4 7.7 %all-to-all-done.7 = f32[32,8,128]{2,1,0:T(8,128)S(1)} async-done(((f32[32,8,128]{2,1,0:T(8,128)}), f32[32,8,128]{2,1,0:T(8,128)S(1)}, u32[]{:S(2)}, u32[]{:S(2)}) %all-to-all-start.7) | async-done | bytes 131104 | tf_op jit(solution)/shard_map/all_to_all | solution.py:701
  166.1 6.7 %shard_map.92 = (f32[2,1024,128]{2,1,0:T(8,128)}, f32[8,128]{1,0:T(8,128)S(1)}, f32[256,128]{1,0:T(8,128)S(1)}) custom-call(f32[256,128]{1,0:T(8,128)S(1)} %bitcast.23, s32[2,4,256]{2,1,0:T(4,128)} %refs_1_.5, bf16[8,64,256]{2,1,0:T(8,128)(2,1)S(1)} %get-tuple-element.66.refs_2_, f32[16,128]{1,0:T(8,128)S(1)} %get-tuple-element.55.refs_6_.refs_3_, ...), custom_call_target="tpu_custom_call" | custom-call | tf_op jit(solution)/shard_map/pallas_call | solution.py:168
  172.8 11.3 %all_to_all.112 = f32[32,8,128]{2,1,0:T(8,128)S(1)} all-to-all(f32[32,8,128]{2,1,0:T(8,128)S(1)} %bitcast.33), channel_id=1, replica_groups={{0,1,16,17,32,33,48,49,64,65,80,81,96,97,112,113,128,129,144,145,160,16..., dimensions={0} | all-to-all | bytes 262144 | tf_op jit(solution)/shard_map/all_to_all | solution.py:701
  184.1 9.2 %all_to_all.113 = f32[8,8,128]{2,1,0:T(8,128)S(1)} all-to-all(f32[8,8,128]{2,1,0:T(8,128)S(1)} %bitcast.30), channel_id=1, replica_groups={{0,2,4,6,8,10,12,14},{1,3,5,7,9,11,13,15},{16,18,20,22,24,26,28,30},{17..., dimensions={0} | all-to-all | bytes 65536 | tf_op jit(solution)/shard_map/all_to_all | solution.py:704
  (39 shorter events, 28.8 us)
Async XLA Ops:
  0.0 11.8 %collective-permute-start.4 = (f32[128,2048]{1,0:T(8,128)}, f32[128,2048]{1,0:T(8,128)S(1)}, u32[]{:S(2)}, u32[]{:S(2)}) collective-permute-start(f32[128,2048]{1,0:T(8,128)} %own.1), channel_id=1, source_target_pairs={{0,1},{1,0},{2,3},{3,2},{4,5},{5,4},{6,7},{7,6},{8,9},{9,8},{10,11... | collective-permute-start | bytes 3145736 | tf_op jit(solution)/shard_map/ppermute | solution.py:707
  5.1 9.9 %collective-permute-start.1 = (f32[2,312,128]{2,1,0:T(8,128)S(1)}, f32[2,312,128]{2,1,0:T(8,128)S(1)}, u32[]{:S(2)}, u32[]{:S(2)}) collective-permute-start(f32[2,312,128]{2,1,0:T(8,128)S(1)} %get-tuple-element.52), channel_id=1, source_target_pairs={{16,32},{48,64},{80,96},{112,128},{144,160},{176,192},{208,224},{3... | collective-permute-start | bytes 958472 | tf_op jit(solution)/shard_map/ppermute | solution.py:265
  5.7 9.7 %collective-permute-start.3 = (f32[2,312,128]{2,1,0:T(8,128)S(1)}, f32[2,312,128]{2,1,0:T(8,128)S(1)}, u32[]{:S(2)}, u32[]{:S(2)}) collective-permute-start(f32[2,312,128]{2,1,0:T(8,128)S(1)} %get-tuple-element.54), channel_id=1, source_target_pairs={{0,16},{32,48},{64,80},{96,112},{128,144},{160,176},{192,208},{224... | collective-permute-start | bytes 958472 | tf_op jit(solution)/shard_map/ppermute | solution.py:266
  7.7 7.2 %collective-permute-start = (f32[312,128]{1,0:T(8,128)S(1)}, f32[312,128]{1,0:T(8,128)S(1)}, u32[]{:S(2)}, u32[]{:S(2)}) collective-permute-start(f32[312,128]{1,0:T(8,128)S(1)} %get-tuple-element.51), channel_id=1, source_target_pairs={{1,2},{3,4},{5,6},{7,8},{9,10},{11,12},{13,14},{2,1},{4,3},{6,5},{... | collective-permute-start | bytes 479240 | tf_op jit(solution)/shard_map/ppermute | solution.py:264
  11.7 3.2 %collective-permute-start.2 = (f32[312,128]{1,0:T(8,128)S(1)}, f32[312,128]{1,0:T(8,128)S(1)}, u32[]{:S(2)}, u32[]{:S(2)}) collective-permute-start(f32[312,128]{1,0:T(8,128)S(1)} %get-tuple-element.53), channel_id=1, source_target_pairs={{0,1},{2,3},{4,5},{6,7},{8,9},{10,11},{12,13},{14,15},{1,0},{3,2},... | collective-permute-start | bytes 479240 | tf_op jit(solution)/shard_map/ppermute | solution.py:267
  38.5 20.5 %all-to-all-start.1 = ((f32[8,72,128]{2,1,0:T(8,128)}), f32[8,72,128]{2,1,0:T(8,128)S(1)}, u32[]{:S(2)}, u32[]{:S(2)}) async-start(f32[8,72,128]{2,1,0:T(8,128)} %bitcast.2), calls=%async_computation.1 | async-start | bytes 589824 | tf_op jit(solution)/shard_map/all_to_all | solution.py:704
  46.7 31.4 %collective-permute-start.6 = (f32[2,256,128]{2,1,0:T(8,128)}, f32[2,256,128]{2,1,0:T(8,128)S(1)}, u32[]{:S(2)}, u32[]{:S(2)}) collective-permute-start(f32[2,256,128]{2,1,0:T(8,128)} %get-tuple-element.70), channel_id=1, source_target_pairs={{16,32},{48,64},{80,96},{112,128},{144,160},{176,192},{208,224},{3... | collective-permute-start | bytes 786440 | tf_op jit(solution)/shard_map/ppermute | solution.py:265
  47.4 30.7 %collective-permute-start.8 = (f32[2,256,128]{2,1,0:T(8,128)}, f32[2,256,128]{2,1,0:T(8,128)S(1)}, u32[]{:S(2)}, u32[]{:S(2)}) collective-permute-start(f32[2,256,128]{2,1,0:T(8,128)} %get-tuple-element.72), channel_id=1, source_target_pairs={{0,16},{32,48},{64,80},{96,112},{128,144},{160,176},{192,208},{224... | collective-permute-start | bytes 786440 | tf_op jit(solution)/shard_map/ppermute | solution.py:266
  60.4 10.1 %all-to-all-start.2 = ((f32[8,8,128]{2,1,0:T(8,128)}), f32[8,8,128]{2,1,0:T(8,128)S(1)}, u32[]{:S(2)}, u32[]{:S(2)}) async-start(f32[8,8,128]{2,1,0:T(8,128)} %bitcast.4), calls=%async_computation.2 | async-start | bytes 65536 | tf_op jit(solution)/shard_map/all_to_all | solution.py:704
  63.7 14.4 %collective-permute-start.5 = (f32[256,128]{1,0:T(8,128)}, f32[256,128]{1,0:T(8,128)S(1)}, u32[]{:S(2)}, u32[]{:S(2)}) collective-permute-start(f32[256,128]{1,0:T(8,128)} %get-tuple-element.69), channel_id=1, source_target_pairs={{1,2},{3,4},{5,6},{7,8},{9,10},{11,12},{13,14},{2,1},{4,3},{6,5},{... | collective-permute-start | bytes 393224 | tf_op jit(solution)/shard_map/ppermute | solution.py:264
  68.3 9.8 %collective-permute-start.7 = (f32[256,128]{1,0:T(8,128)}, f32[256,128]{1,0:T(8,128)S(1)}, u32[]{:S(2)}, u32[]{:S(2)}) collective-permute-start(f32[256,128]{1,0:T(8,128)} %get-tuple-element.71), channel_id=1, source_target_pairs={{0,1},{2,3},{4,5},{6,7},{8,9},{10,11},{12,13},{14,15},{1,0},{3,2},... | collective-permute-start | bytes 393224 | tf_op jit(solution)/shard_map/ppermute | solution.py:267
  72.2 13.7 %all-to-all-start.3 = ((f32[32,8,128]{2,1,0:T(8,128)}), f32[32,8,128]{2,1,0:T(8,128)S(1)}, u32[]{:S(2)}, u32[]{:S(2)}) async-start(f32[32,8,128]{2,1,0:T(8,128)} %bitcast.6), calls=%async_computation.3 | async-start | bytes 262144 | tf_op jit(solution)/shard_map/all_to_all | solution.py:701
  94.6 20.0 %collective-permute-start.10 = (f32[2,256,128]{2,1,0:T(8,128)}, f32[2,256,128]{2,1,0:T(8,128)S(1)}, u32[]{:S(2)}, u32[]{:S(2)}) collective-permute-start(f32[2,256,128]{2,1,0:T(8,128)} %get-tuple-element.77), channel_id=1, source_target_pairs={{16,32},{48,64},{80,96},{112,128},{144,160},{176,192},{208,224},{3... | collective-permute-start | bytes 786440 | tf_op jit(solution)/shard_map/ppermute | solution.py:265
  95.3 19.3 %collective-permute-start.12 = (f32[2,256,128]{2,1,0:T(8,128)}, f32[2,256,128]{2,1,0:T(8,128)S(1)}, u32[]{:S(2)}, u32[]{:S(2)}) collective-permute-start(f32[2,256,128]{2,1,0:T(8,128)} %get-tuple-element.79), channel_id=1, source_target_pairs={{0,16},{32,48},{64,80},{96,112},{128,144},{160,176},{192,208},{224... | collective-permute-start | bytes 786440 | tf_op jit(solution)/shard_map/ppermute | solution.py:266
  97.1 17.5 %collective-permute-start.9 = (f32[256,128]{1,0:T(8,128)}, f32[256,128]{1,0:T(8,128)S(1)}, u32[]{:S(2)}, u32[]{:S(2)}) collective-permute-start(f32[256,128]{1,0:T(8,128)} %get-tuple-element.76), channel_id=1, source_target_pairs={{1,2},{3,4},{5,6},{7,8},{9,10},{11,12},{13,14},{2,1},{4,3},{6,5},{... | collective-permute-start | bytes 393224 | tf_op jit(solution)/shard_map/ppermute | solution.py:264
  100.0 14.6 %collective-permute-start.11 = (f32[256,128]{1,0:T(8,128)}, f32[256,128]{1,0:T(8,128)S(1)}, u32[]{:S(2)}, u32[]{:S(2)}) collective-permute-start(f32[256,128]{1,0:T(8,128)} %get-tuple-element.78), channel_id=1, source_target_pairs={{0,1},{2,3},{4,5},{6,7},{8,9},{10,11},{12,13},{14,15},{1,0},{3,2},... | collective-permute-start | bytes 393224 | tf_op jit(solution)/shard_map/ppermute | solution.py:267
  123.6 16.4 %all-to-all-start.5 = ((f32[8,72,128]{2,1,0:T(8,128)}), f32[8,72,128]{2,1,0:T(8,128)S(1)}, u32[]{:S(2)}, u32[]{:S(2)}) async-start(f32[8,72,128]{2,1,0:T(8,128)} %bitcast.10), calls=%async_computation.5 | async-start | bytes 589824 | tf_op jit(solution)/shard_map/all_to_all | solution.py:704
  127.0 31.3 %collective-permute-start.14 = (f32[2,256,128]{2,1,0:T(8,128)}, f32[2,256,128]{2,1,0:T(8,128)S(1)}, u32[]{:S(2)}, u32[]{:S(2)}) collective-permute-start(f32[2,256,128]{2,1,0:T(8,128)} %get-tuple-element.86), channel_id=1, source_target_pairs={{16,32},{48,64},{80,96},{112,128},{144,160},{176,192},{208,224},{3... | collective-permute-start | bytes 786440 | tf_op jit(solution)/shard_map/ppermute | solution.py:265
  127.7 30.7 %collective-permute-start.16 = (f32[2,256,128]{2,1,0:T(8,128)}, f32[2,256,128]{2,1,0:T(8,128)S(1)}, u32[]{:S(2)}, u32[]{:S(2)}) collective-permute-start(f32[2,256,128]{2,1,0:T(8,128)} %get-tuple-element.88), channel_id=1, source_target_pairs={{0,16},{32,48},{64,80},{96,112},{128,144},{160,176},{192,208},{224... | collective-permute-start | bytes 786440 | tf_op jit(solution)/shard_map/ppermute | solution.py:266
  141.3 10.1 %all-to-all-start.6 = ((f32[8,8,128]{2,1,0:T(8,128)}), f32[8,8,128]{2,1,0:T(8,128)S(1)}, u32[]{:S(2)}, u32[]{:S(2)}) async-start(f32[8,8,128]{2,1,0:T(8,128)} %bitcast.12), calls=%async_computation.6 | async-start | bytes 65536 | tf_op jit(solution)/shard_map/all_to_all | solution.py:704
  144.6 13.7 %collective-permute-start.13 = (f32[256,128]{1,0:T(8,128)}, f32[256,128]{1,0:T(8,128)S(1)}, u32[]{:S(2)}, u32[]{:S(2)}) collective-permute-start(f32[256,128]{1,0:T(8,128)} %get-tuple-element.85), channel_id=1, source_target_pairs={{1,2},{3,4},{5,6},{7,8},{9,10},{11,12},{13,14},{2,1},{4,3},{6,5},{... | collective-permute-start | bytes 393224 | tf_op jit(solution)/shard_map/ppermute | solution.py:264
  148.5 9.8 %collective-permute-start.15 = (f32[256,128]{1,0:T(8,128)}, f32[256,128]{1,0:T(8,128)S(1)}, u32[]{:S(2)}, u32[]{:S(2)}) collective-permute-start(f32[256,128]{1,0:T(8,128)} %get-tuple-element.87), channel_id=1, source_target_pairs={{0,1},{2,3},{4,5},{6,7},{8,9},{10,11},{12,13},{14,15},{1,0},{3,2},... | collective-permute-start | bytes 393224 | tf_op jit(solution)/shard_map/ppermute | solution.py:267
  153.1 13.0 %all-to-all-start.7 = ((f32[32,8,128]{2,1,0:T(8,128)}), f32[32,8,128]{2,1,0:T(8,128)S(1)}, u32[]{:S(2)}, u32[]{:S(2)}) async-start(f32[32,8,128]{2,1,0:T(8,128)} %bitcast.14), calls=%async_computation.7 | async-start | bytes 262144 | tf_op jit(solution)/shard_map/all_to_all | solution.py:701
where the time goes:
time: 197 us; the launch traced here: 196 us
  starting transfers between devices  58.7 us (30%)
  blocking collectives  51 us (26%)
  Pallas kernels  44.2 us (22%)
  waiting for transfers between devices  41.5 us (21%)
    all_to_all x3, blocking collectives, to_owners(): lax.all_to_all(value, AXES, 0, 0, axis_index_groups=plane, tiled=True)  41.8 us
    pallas_call x12, Pallas kernels, call(): pl.pallas_call(whole, out_shape=[pltpu.HBM(out.shape, out.dtype) if isins...  41.7 us
    all_to_all x4, waiting for transfers between devices, along_z(): lax.all_to_all(value, AXES, 0, 0, axis_index_groups=column, tiled=True)  25.1 us
    all_to_all x4, starting transfers between devices, along_z(): lax.all_to_all(value, AXES, 0, 0, axis_index_groups=column, tiled=True)  18.3 us
    ppermute x4, starting transfers between devices, exchange(): other_core = lax.ppermute(other_core, 'sub', pairs(n_sub, 1))  15.4 us
    all_to_all x2, waiting for transfers between devices, to_owners(): lax.all_to_all(value, AXES, 0, 0, axis_index_groups=plane, tiled=True)  15.4 us
    all_to_all x2, starting transfers between devices, to_owners(): lax.all_to_all(value, AXES, 0, 0, axis_index_groups=plane, tiled=True)  11.2 us
    all_to_all x1, blocking collectives, along_z(): lax.all_to_all(value, AXES, 0, 0, axis_index_groups=column, tiled=True)  9.24 us
  transfers between devices with their start and end apart: 23, of which 8 were waited for; matrix products, arithmetic and copies ran while one was open for 0% of the time, Pallas kernels for 5%

commit v1 on v0

--- a/solution.py
+++ b/solution.py
@@ -755,14 +755,14 @@
         direction_kernel,
         [vector, vector, message_shape] + halo_shapes(FACE, Far),
         returned, dof_order, traces, weights, local, *recv, loads, schur,
-        far=[1] + list(range(4, 12)), loose=range(6, 10), scratch=(one_hot,),
+        far=[1, 4, 5, 10, 11], scratch=(one_hot,),
     )
     recv = halo(faces)
     gathered, local, *faces = call(
         image_kernel,
         [gathered_shape, vector] + halo_shapes(FACE, Far),
         to_owners(message), maps, dof_order, weights, partial, *recv, neumann,
-        far=[2] + list(range(4, 11)), loose=range(6, 10), scratch=lists + (one_hot,),
+        far=[2, 4, 5, 10], scratch=lists + (one_hot,),
     )
     recv = halo(faces)
     returned = coarse_solve(gathered, maps)
@@ -770,7 +770,7 @@
         last_kernel,
         [vector, small, message_shape],
         returned, dof_order, traces, weights, local, *recv, direction, loads, schur,
-        far=[1] + list(range(4, 13)), loose=range(6, 10), scratch=(one_hot,),
+        far=[1, 4, 5, 10, 11, 12], scratch=(one_hot,),
     )
     (sums,) = call(sum_kernel, [Near((n_z * TILE, LANES))], to_owners(message))
     (out,) = call(

time: 197 us -> 196 us (level)
  no operation moved by 1% of the time
where the time goes in v1:
time: 196 us; the launch traced here: 195 us
  starting transfers between devices  58.7 us (30%)
  blocking collectives  51 us (26%)
  Pallas kernels  43.5 us (22%)
  waiting for transfers between devices  41.5 us (21%)
    all_to_all x3, blocking collectives, to_owners(): lax.all_to_all(value, AXES, 0, 0, axis_index_groups=plane, tiled=True)  41.8 us
    pallas_call x12, Pallas kernels, call(): pl.pallas_call(whole, out_shape=[pltpu.HBM(out.shape, out.dtype) if isins...  40.9 us
    all_to_all x4, waiting for transfers between devices, along_z(): lax.all_to_all(value, AXES, 0, 0, axis_index_groups=column, tiled=True)  25.1 us
    all_to_all x4, starting transfers between devices, along_z(): lax.all_to_all(value, AXES, 0, 0, axis_index_groups=column, tiled=True)  18.3 us
    ppermute x4, starting transfers between devices, exchange(): other_core = lax.ppermute(other_core, 'sub', pairs(n_sub, 1))  15.4 us
    all_to_all x2, waiting for transfers between devices, to_owners(): lax.all_to_all(value, AXES, 0, 0, axis_index_groups=plane, tiled=True)  15.4 us
    all_to_all x2, starting transfers between devices, to_owners(): lax.all_to_all(value, AXES, 0, 0, axis_index_groups=plane, tiled=True)  11.2 us
    all_to_all x1, blocking collectives, along_z(): lax.all_to_all(value, AXES, 0, 0, axis_index_groups=column, tiled=True)  9.24 us
  transfers between devices with their start and end apart: 23, of which 8 were waited for; matrix products, arithmetic and copies ran while one was open for 0% of the time, Pallas kernels for 5%

profile of v1, /device:TPU:1, one launch (start us, length us, event | category | flops | bytes accessed | tf_op | source)
XLA Modules:
  0.0 195.2 jit_solution(5194405000658998433)
XLA Ops:
  0.0 3.2 %collective-permute-start.4 = (f32[128,2048]{1,0:T(8,128)}, f32[128,2048]{1,0:T(8,128)S(1)}, u32[]{:S(2)}, u32[]{:S(2)}) collective-permute-start(f32[128,2048]{1,0:T(8,128)} %own.1), channel_id=1, source_target_pairs={{0,1},{1,0},{2,3},{3,2},{4,5},{5,4},{6,7},{7,6},{8,9},{9,8},{10,11... | collective-permute-start | bytes 3145736 | tf_op jit(solution)/shard_map/ppermute | solution.py:707
  7.7 4.0 %collective-permute-start = (f32[312,128]{1,0:T(8,128)S(1)}, f32[312,128]{1,0:T(8,128)S(1)}, u32[]{:S(2)}, u32[]{:S(2)}) collective-permute-start(f32[312,128]{1,0:T(8,128)S(1)} %get-tuple-element.51), channel_id=1, source_target_pairs={{1,2},{3,4},{5,6},{7,8},{9,10},{11,12},{13,14},{2,1},{4,3},{6,5},{... | collective-permute-start | bytes 479240 | tf_op jit(solution)/shard_map/ppermute | solution.py:264
  15.5 4.7 %shard_map.84 = (f32[2,1024,128]{2,1,0:T(8,128)}, bf16[8,64,256]{2,1,0:T(8,128)(2,1)S(1)}, f32[256,128]{1,0:T(8,128)S(1)}, f32[2,256,128]{2,1,0:T(8,128)}, f32[2...) custom-call(bf16[8,256,256]{2,1,0:T(8,128)(2,1)S(1)} %get-tuple-element.49.refs_0_, ...), custom_call_target="tpu_custom_call" | custom-call | tf_op jit(solution)/shard_map/pallas_call | solution.py:168
  20.2 16.1 %all_to_all.110 = f32[32,8,128]{2,1,0:T(8,128)S(1)} all-to-all(f32[32,8,128]{2,1,0:T(8,128)S(1)} %bitcast.32), channel_id=1, replica_groups={{0,1,16,17,32,33,48,49,64,65,80,81,96,97,112,113,128,129,144,145,160,16..., dimensions={0} | all-to-all | bytes 262144 | tf_op jit(solution)/shard_map/all_to_all | solution.py:701
  38.5 8.2 %all-to-all-start.1 = ((f32[8,72,128]{2,1,0:T(8,128)}), f32[8,72,128]{2,1,0:T(8,128)S(1)}, u32[]{:S(2)}, u32[]{:S(2)}) async-start(f32[8,72,128]{2,1,0:T(8,128)} %bitcast.2), calls=%async_computation.1 | async-start | bytes 589824 | tf_op jit(solution)/shard_map/all_to_all | solution.py:704
  49.2 9.9 %all-to-all-done.1 = f32[8,72,128]{2,1,0:T(8,128)S(1)} async-done(((f32[8,72,128]{2,1,0:T(8,128)}), f32[8,72,128]{2,1,0:T(8,128)S(1)}, u32[]{:S(2)}, u32[]{:S(2)}) %all-to-all-start.1) | async-done | bytes 294944 | tf_op jit(solution)/shard_map/all_to_all | solution.py:704
  60.4 3.3 %all-to-all-start.2 = ((f32[8,8,128]{2,1,0:T(8,128)}), f32[8,8,128]{2,1,0:T(8,128)S(1)}, u32[]{:S(2)}, u32[]{:S(2)}) async-start(f32[8,8,128]{2,1,0:T(8,128)} %bitcast.4), calls=%async_computation.2 | async-start | bytes 65536 | tf_op jit(solution)/shard_map/all_to_all | solution.py:704
  63.7 4.6 %collective-permute-start.5 = (f32[256,128]{1,0:T(8,128)}, f32[256,128]{1,0:T(8,128)S(1)}, u32[]{:S(2)}, u32[]{:S(2)}) collective-permute-start(f32[256,128]{1,0:T(8,128)} %get-tuple-element.69), channel_id=1, source_target_pairs={{1,2},{3,4},{5,6},{7,8},{9,10},{11,12},{13,14},{2,1},{4,3},{6,5},{... | collective-permute-start | bytes 393224 | tf_op jit(solution)/shard_map/ppermute | solution.py:264
  72.2 5.9 %all-to-all-start.3 = ((f32[32,8,128]{2,1,0:T(8,128)}), f32[32,8,128]{2,1,0:T(8,128)S(1)}, u32[]{:S(2)}, u32[]{:S(2)}) async-start(f32[32,8,128]{2,1,0:T(8,128)} %bitcast.6), calls=%async_computation.3 | async-start | bytes 262144 | tf_op jit(solution)/shard_map/all_to_all | solution.py:701
  78.2 7.7 %all-to-all-done.3 = f32[32,8,128]{2,1,0:T(8,128)S(1)} async-done(((f32[32,8,128]{2,1,0:T(8,128)}), f32[32,8,128]{2,1,0:T(8,128)S(1)}, u32[]{:S(2)}, u32[]{:S(2)}) %all-to-all-start.3) | async-done | bytes 131104 | tf_op jit(solution)/shard_map/all_to_all | solution.py:701
  85.9 8.5 %shard_map.88 = (f32[2,1024,128]{2,1,0:T(8,128)}, f32[2,1024,128]{2,1,0:T(8,128)}, f32[256,128]{1,0:T(8,128)S(1)}, f32[2,256,128]{2,1,0:T(8,128)}, f32[2,256,128...) custom-call(f32[256,128]{1,0:T(8,128)S(1)} %bitcast.22, s32[2,4,256]{2,1,0:T(4,128)} %refs_1_.5, ...), custom_call_target="tpu_custom_call" | custom-call | tf_op jit(solution)/shard_map/pallas_call | solution.py:168
  96.8 2.9 %collective-permute-start.9 = (f32[256,128]{1,0:T(8,128)}, f32[256,128]{1,0:T(8,128)S(1)}, u32[]{:S(2)}, u32[]{:S(2)}) collective-permute-start(f32[256,128]{1,0:T(8,128)} %get-tuple-element.76), channel_id=1, source_target_pairs={{1,2},{3,4},{5,6},{7,8},{9,10},{11,12},{13,14},{2,1},{4,3},{6,5},{... | collective-permute-start | bytes 393224 | tf_op jit(solution)/shard_map/ppermute | solution.py:264
  99.9 14.5 %all_to_all.111 = f32[32,8,128]{2,1,0:T(8,128)S(1)} all-to-all(f32[32,8,128]{2,1,0:T(8,128)S(1)} %bitcast.31), channel_id=1, replica_groups={{0,1,16,17,32,33,48,49,64,65,80,81,96,97,112,113,128,129,144,145,160,16..., dimensions={0} | all-to-all | bytes 262144 | tf_op jit(solution)/shard_map/all_to_all | solution.py:701
  114.3 8.8 %shard_map.89 = (f32[576,128]{1,0:T(8,128)}, f32[2,1024,128]{2,1,0:T(8,128)}, f32[2,256,128]{2,1,0:T(8,128)}, f32[2,256,128]{2,1,0:T(8,128)}, f32[256,128]{1,0:T...) custom-call(f32[256,128]{1,0:T(8,128)S(1)} %bitcast.24, f32[64,128]{1,0:T(8,128)S(1)} %get-tuple-element.64.refs_1_, ...), custom_call_target="tpu_custom_call" | custom-call | tf_op jit(solution)/shard_map/pallas_call | solution.py:168
  123.1 3.4 %all-to-all-start.5 = ((f32[8,72,128]{2,1,0:T(8,128)}), f32[8,72,128]{2,1,0:T(8,128)S(1)}, u32[]{:S(2)}, u32[]{:S(2)}) async-start(f32[8,72,128]{2,1,0:T(8,128)} %bitcast.10), calls=%async_computation.5 | async-start | bytes 589824 | tf_op jit(solution)/shard_map/all_to_all | solution.py:704
  129.0 10.5 %all-to-all-done.5 = f32[8,72,128]{2,1,0:T(8,128)S(1)} async-done(((f32[8,72,128]{2,1,0:T(8,128)}), f32[8,72,128]{2,1,0:T(8,128)S(1)}, u32[]{:S(2)}, u32[]{:S(2)}) %all-to-all-start.5) | async-done | bytes 294944 | tf_op jit(solution)/shard_map/all_to_all | solution.py:704
  140.8 3.3 %all-to-all-start.6 = ((f32[8,8,128]{2,1,0:T(8,128)}), f32[8,8,128]{2,1,0:T(8,128)S(1)}, u32[]{:S(2)}, u32[]{:S(2)}) async-start(f32[8,8,128]{2,1,0:T(8,128)} %bitcast.12), calls=%async_computation.6 | async-start | bytes 65536 | tf_op jit(solution)/shard_map/all_to_all | solution.py:704
  144.2 3.9 %collective-permute-start.13 = (f32[256,128]{1,0:T(8,128)}, f32[256,128]{1,0:T(8,128)S(1)}, u32[]{:S(2)}, u32[]{:S(2)}) collective-permute-start(f32[256,128]{1,0:T(8,128)} %get-tuple-element.85), channel_id=1, source_target_pairs={{1,2},{3,4},{5,6},{7,8},{9,10},{11,12},{13,14},{2,1},{4,3},{6,5},{... | collective-permute-start | bytes 393224 | tf_op jit(solution)/shard_map/ppermute | solution.py:264
  148.4 2.6 %all-to-all-done.6 = f32[8,8,128]{2,1,0:T(8,128)S(1)} async-done(((f32[8,8,128]{2,1,0:T(8,128)}), f32[8,8,128]{2,1,0:T(8,128)S(1)}, u32[]{:S(2)}, u32[]{:S(2)}) %all-to-all-start.6) | async-done | bytes 32800 | tf_op jit(solution)/shard_map/all_to_all | solution.py:704
  152.7 5.2 %all-to-all-start.7 = ((f32[32,8,128]{2,1,0:T(8,128)}), f32[32,8,128]{2,1,0:T(8,128)S(1)}, u32[]{:S(2)}, u32[]{:S(2)}) async-start(f32[32,8,128]{2,1,0:T(8,128)} %bitcast.14), calls=%async_computation.7 | async-start | bytes 262144 | tf_op jit(solution)/shard_map/all_to_all | solution.py:701
  157.9 7.7 %all-to-all-done.7 = f32[32,8,128]{2,1,0:T(8,128)S(1)} async-done(((f32[32,8,128]{2,1,0:T(8,128)}), f32[32,8,128]{2,1,0:T(8,128)S(1)}, u32[]{:S(2)}, u32[]{:S(2)}) %all-to-all-start.7) | async-done | bytes 131104 | tf_op jit(solution)/shard_map/all_to_all | solution.py:701
  165.6 6.4 %shard_map.92 = (f32[2,1024,128]{2,1,0:T(8,128)}, f32[8,128]{1,0:T(8,128)S(1)}, f32[256,128]{1,0:T(8,128)S(1)}) custom-call(f32[256,128]{1,0:T(8,128)S(1)} %bitcast.23, s32[2,4,256]{2,1,0:T(4,128)} %refs_1_.5, bf16[8,64,256]{2,1,0:T(8,128)(2,1)S(1)} %get-tuple-element.66.refs_2_, f32[16,128]{1,0:T(8,128)S(1)} %get-tuple-element.55.refs_6_.refs_3_, ...), custom_call_target="tpu_custom_call" | custom-call | tf_op jit(solution)/shard_map/pallas_call | solution.py:168
  172.1 11.3 %all_to_all.112 = f32[32,8,128]{2,1,0:T(8,128)S(1)} all-to-all(f32[32,8,128]{2,1,0:T(8,128)S(1)} %bitcast.33), channel_id=1, replica_groups={{0,1,16,17,32,33,48,49,64,65,80,81,96,97,112,113,128,129,144,145,160,16..., dimensions={0} | all-to-all | bytes 262144 | tf_op jit(solution)/shard_map/all_to_all | solution.py:701
  183.4 9.2 %all_to_all.113 = f32[8,8,128]{2,1,0:T(8,128)S(1)} all-to-all(f32[8,8,128]{2,1,0:T(8,128)S(1)} %bitcast.30), channel_id=1, replica_groups={{0,2,4,6,8,10,12,14},{1,3,5,7,9,11,13,15},{16,18,20,22,24,26,28,30},{17..., dimensions={0} | all-to-all | bytes 65536 | tf_op jit(solution)/shard_map/all_to_all | solution.py:704
  (39 shorter events, 28.8 us)
Async XLA Ops:
  0.0 11.8 %collective-permute-start.4 = (f32[128,2048]{1,0:T(8,128)}, f32[128,2048]{1,0:T(8,128)S(1)}, u32[]{:S(2)}, u32[]{:S(2)}) collective-permute-start(f32[128,2048]{1,0:T(8,128)} %own.1), channel_id=1, source_target_pairs={{0,1},{1,0},{2,3},{3,2},{4,5},{5,4},{6,7},{7,6},{8,9},{9,8},{10,11... | collective-permute-start | bytes 3145736 | tf_op jit(solution)/shard_map/ppermute | solution.py:707
  5.1 9.9 %collective-permute-start.1 = (f32[2,312,128]{2,1,0:T(8,128)S(1)}, f32[2,312,128]{2,1,0:T(8,128)S(1)}, u32[]{:S(2)}, u32[]{:S(2)}) collective-permute-start(f32[2,312,128]{2,1,0:T(8,128)S(1)} %get-tuple-element.52), channel_id=1, source_target_pairs={{16,32},{48,64},{80,96},{112,128},{144,160},{176,192},{208,224},{3... | collective-permute-start | bytes 958472 | tf_op jit(solution)/shard_map/ppermute | solution.py:265
  5.7 9.7 %collective-permute-start.3 = (f32[2,312,128]{2,1,0:T(8,128)S(1)}, f32[2,312,128]{2,1,0:T(8,128)S(1)}, u32[]{:S(2)}, u32[]{:S(2)}) collective-permute-start(f32[2,312,128]{2,1,0:T(8,128)S(1)} %get-tuple-element.54), channel_id=1, source_target_pairs={{0,16},{32,48},{64,80},{96,112},{128,144},{160,176},{192,208},{224... | collective-permute-start | bytes 958472 | tf_op jit(solution)/shard_map/ppermute | solution.py:266
  7.7 7.2 %collective-permute-start = (f32[312,128]{1,0:T(8,128)S(1)}, f32[312,128]{1,0:T(8,128)S(1)}, u32[]{:S(2)}, u32[]{:S(2)}) collective-permute-start(f32[312,128]{1,0:T(8,128)S(1)} %get-tuple-element.51), channel_id=1, source_target_pairs={{1,2},{3,4},{5,6},{7,8},{9,10},{11,12},{13,14},{2,1},{4,3},{6,5},{... | collective-permute-start | bytes 479240 | tf_op jit(solution)/shard_map/ppermute | solution.py:264
  11.7 3.2 %collective-permute-start.2 = (f32[312,128]{1,0:T(8,128)S(1)}, f32[312,128]{1,0:T(8,128)S(1)}, u32[]{:S(2)}, u32[]{:S(2)}) collective-permute-start(f32[312,128]{1,0:T(8,128)S(1)} %get-tuple-element.53), channel_id=1, source_target_pairs={{0,1},{2,3},{4,5},{6,7},{8,9},{10,11},{12,13},{14,15},{1,0},{3,2},... | collective-permute-start | bytes 479240 | tf_op jit(solution)/shard_map/ppermute | solution.py:267
  38.5 20.5 %all-to-all-start.1 = ((f32[8,72,128]{2,1,0:T(8,128)}), f32[8,72,128]{2,1,0:T(8,128)S(1)}, u32[]{:S(2)}, u32[]{:S(2)}) async-start(f32[8,72,128]{2,1,0:T(8,128)} %bitcast.2), calls=%async_computation.1 | async-start | bytes 589824 | tf_op jit(solution)/shard_map/all_to_all | solution.py:704
  46.7 31.4 %collective-permute-start.6 = (f32[2,256,128]{2,1,0:T(8,128)}, f32[2,256,128]{2,1,0:T(8,128)S(1)}, u32[]{:S(2)}, u32[]{:S(2)}) collective-permute-start(f32[2,256,128]{2,1,0:T(8,128)} %get-tuple-element.70), channel_id=1, source_target_pairs={{16,32},{48,64},{80,96},{112,128},{144,160},{176,192},{208,224},{3... | collective-permute-start | bytes 786440 | tf_op jit(solution)/shard_map/ppermute | solution.py:265
  47.4 30.7 %collective-permute-start.8 = (f32[2,256,128]{2,1,0:T(8,128)}, f32[2,256,128]{2,1,0:T(8,128)S(1)}, u32[]{:S(2)}, u32[]{:S(2)}) collective-permute-start(f32[2,256,128]{2,1,0:T(8,128)} %get-tuple-element.72), channel_id=1, source_target_pairs={{0,16},{32,48},{64,80},{96,112},{128,144},{160,176},{192,208},{224... | collective-permute-start | bytes 786440 | tf_op jit(solution)/shard_map/ppermute | solution.py:266
  60.4 10.1 %all-to-all-start.2 = ((f32[8,8,128]{2,1,0:T(8,128)}), f32[8,8,128]{2,1,0:T(8,128)S(1)}, u32[]{:S(2)}, u32[]{:S(2)}) async-start(f32[8,8,128]{2,1,0:T(8,128)} %bitcast.4), calls=%async_computation.2 | async-start | bytes 65536 | tf_op jit(solution)/shard_map/all_to_all | solution.py:704
  63.7 14.4 %collective-permute-start.5 = (f32[256,128]{1,0:T(8,128)}, f32[256,128]{1,0:T(8,128)S(1)}, u32[]{:S(2)}, u32[]{:S(2)}) collective-permute-start(f32[256,128]{1,0:T(8,128)} %get-tuple-element.69), channel_id=1, source_target_pairs={{1,2},{3,4},{5,6},{7,8},{9,10},{11,12},{13,14},{2,1},{4,3},{6,5},{... | collective-permute-start | bytes 393224 | tf_op jit(solution)/shard_map/ppermute | solution.py:264
  68.3 9.8 %collective-permute-start.7 = (f32[256,128]{1,0:T(8,128)}, f32[256,128]{1,0:T(8,128)S(1)}, u32[]{:S(2)}, u32[]{:S(2)}) collective-permute-start(f32[256,128]{1,0:T(8,128)} %get-tuple-element.71), channel_id=1, source_target_pairs={{0,1},{2,3},{4,5},{6,7},{8,9},{10,11},{12,13},{14,15},{1,0},{3,2},... | collective-permute-start | bytes 393224 | tf_op jit(solution)/shard_map/ppermute | solution.py:267
  72.2 13.7 %all-to-all-start.3 = ((f32[32,8,128]{2,1,0:T(8,128)}), f32[32,8,128]{2,1,0:T(8,128)S(1)}, u32[]{:S(2)}, u32[]{:S(2)}) async-start(f32[32,8,128]{2,1,0:T(8,128)} %bitcast.6), calls=%async_computation.3 | async-start | bytes 262144 | tf_op jit(solution)/shard_map/all_to_all | solution.py:701
  94.4 20.0 %collective-permute-start.10 = (f32[2,256,128]{2,1,0:T(8,128)}, f32[2,256,128]{2,1,0:T(8,128)S(1)}, u32[]{:S(2)}, u32[]{:S(2)}) collective-permute-start(f32[2,256,128]{2,1,0:T(8,128)} %get-tuple-element.77), channel_id=1, source_target_pairs={{16,32},{48,64},{80,96},{112,128},{144,160},{176,192},{208,224},{3... | collective-permute-start | bytes 786440 | tf_op jit(solution)/shard_map/ppermute | solution.py:265
  95.0 19.3 %collective-permute-start.12 = (f32[2,256,128]{2,1,0:T(8,128)}, f32[2,256,128]{2,1,0:T(8,128)S(1)}, u32[]{:S(2)}, u32[]{:S(2)}) collective-permute-start(f32[2,256,128]{2,1,0:T(8,128)} %get-tuple-element.79), channel_id=1, source_target_pairs={{0,16},{32,48},{64,80},{96,112},{128,144},{160,176},{192,208},{224... | collective-permute-start | bytes 786440 | tf_op jit(solution)/shard_map/ppermute | solution.py:266
  96.8 17.5 %collective-permute-start.9 = (f32[256,128]{1,0:T(8,128)}, f32[256,128]{1,0:T(8,128)S(1)}, u32[]{:S(2)}, u32[]{:S(2)}) collective-permute-start(f32[256,128]{1,0:T(8,128)} %get-tuple-element.76), channel_id=1, source_target_pairs={{1,2},{3,4},{5,6},{7,8},{9,10},{11,12},{13,14},{2,1},{4,3},{6,5},{... | collective-permute-start | bytes 393224 | tf_op jit(solution)/shard_map/ppermute | solution.py:264
  99.8 14.6 %collective-permute-start.11 = (f32[256,128]{1,0:T(8,128)}, f32[256,128]{1,0:T(8,128)S(1)}, u32[]{:S(2)}, u32[]{:S(2)}) collective-permute-start(f32[256,128]{1,0:T(8,128)} %get-tuple-element.78), channel_id=1, source_target_pairs={{0,1},{2,3},{4,5},{6,7},{8,9},{10,11},{12,13},{14,15},{1,0},{3,2},... | collective-permute-start | bytes 393224 | tf_op jit(solution)/shard_map/ppermute | solution.py:267
  123.1 16.4 %all-to-all-start.5 = ((f32[8,72,128]{2,1,0:T(8,128)}), f32[8,72,128]{2,1,0:T(8,128)S(1)}, u32[]{:S(2)}, u32[]{:S(2)}) async-start(f32[8,72,128]{2,1,0:T(8,128)} %bitcast.10), calls=%async_computation.5 | async-start | bytes 589824 | tf_op jit(solution)/shard_map/all_to_all | solution.py:704
  126.6 31.3 %collective-permute-start.14 = (f32[2,256,128]{2,1,0:T(8,128)}, f32[2,256,128]{2,1,0:T(8,128)S(1)}, u32[]{:S(2)}, u32[]{:S(2)}) collective-permute-start(f32[2,256,128]{2,1,0:T(8,128)} %get-tuple-element.86), channel_id=1, source_target_pairs={{16,32},{48,64},{80,96},{112,128},{144,160},{176,192},{208,224},{3... | collective-permute-start | bytes 786440 | tf_op jit(solution)/shard_map/ppermute | solution.py:265
  127.3 30.7 %collective-permute-start.16 = (f32[2,256,128]{2,1,0:T(8,128)}, f32[2,256,128]{2,1,0:T(8,128)S(1)}, u32[]{:S(2)}, u32[]{:S(2)}) collective-permute-start(f32[2,256,128]{2,1,0:T(8,128)} %get-tuple-element.88), channel_id=1, source_target_pairs={{0,16},{32,48},{64,80},{96,112},{128,144},{160,176},{192,208},{224... | collective-permute-start | bytes 786440 | tf_op jit(solution)/shard_map/ppermute | solution.py:266
  140.8 10.1 %all-to-all-start.6 = ((f32[8,8,128]{2,1,0:T(8,128)}), f32[8,8,128]{2,1,0:T(8,128)S(1)}, u32[]{:S(2)}, u32[]{:S(2)}) async-start(f32[8,8,128]{2,1,0:T(8,128)} %bitcast.12), calls=%async_computation.6 | async-start | bytes 65536 | tf_op jit(solution)/shard_map/all_to_all | solution.py:704
  144.2 13.7 %collective-permute-start.13 = (f32[256,128]{1,0:T(8,128)}, f32[256,128]{1,0:T(8,128)S(1)}, u32[]{:S(2)}, u32[]{:S(2)}) collective-permute-start(f32[256,128]{1,0:T(8,128)} %get-tuple-element.85), channel_id=1, source_target_pairs={{1,2},{3,4},{5,6},{7,8},{9,10},{11,12},{13,14},{2,1},{4,3},{6,5},{... | collective-permute-start | bytes 393224 | tf_op jit(solution)/shard_map/ppermute | solution.py:264
  148.1 9.8 %collective-permute-start.15 = (f32[256,128]{1,0:T(8,128)}, f32[256,128]{1,0:T(8,128)S(1)}, u32[]{:S(2)}, u32[]{:S(2)}) collective-permute-start(f32[256,128]{1,0:T(8,128)} %get-tuple-element.87), channel_id=1, source_target_pairs={{0,1},{2,3},{4,5},{6,7},{8,9},{10,11},{12,13},{14,15},{1,0},{3,2},... | collective-permute-start | bytes 393224 | tf_op jit(solution)/shard_map/ppermute | solution.py:267
  152.7 13.0 %all-to-all-start.7 = ((f32[32,8,128]{2,1,0:T(8,128)}), f32[32,8,128]{2,1,0:T(8,128)S(1)}, u32[]{:S(2)}, u32[]{:S(2)}) async-start(f32[32,8,128]{2,1,0:T(8,128)} %bitcast.14), calls=%async_computation.7 | async-start | bytes 262144 | tf_op jit(solution)/shard_map/all_to_all | solution.py:701

commit v2 on v1

--- a/solution.py
+++ b/solution.py
@@ -454,6 +454,10 @@
     scatter(received, received, lambda d, k: TILE * d + COLS + k, gathered, lhs, hot, 1)
 
 
+def scatter_both_kernel(received, maps, gathered, lhs, hot):
+    scatter(received, maps, lambda d, k: 2 * d + k, gathered, lhs, hot, 2)
+
+
 def coarse_kernel(gathered, high, low, slab, scalars):
     n_z = gathered.shape[0] // GATHER
     total = gathered[pl.ds(0, GATHER), :]
@@ -564,13 +568,12 @@
 
 
 def image_kernel(
-    received, maps, dof, weights, partial, inside, other_core, other_slab, core, slab, neumann,
-    gathered, local, *rest,
+    received, dof, weights, partial, inside, other_core, other_slab, core, slab, neumann,
+    local, *rest,
 ):
-    faces, (lhs, hot, order) = rest[:5], rest[5:]
+    faces, order = rest[:5], rest[5]
     put_order(order, dof)
     recv = (slab, other_slab, core, other_core, inside)
-    scatter(received, maps, lambda d, k: 2 * d + k, gathered, lhs, hot, 2)
 
     def canon(s, f):
         return to_canon(order[4 * s + f], local[s, rows(f), :])
@@ -758,11 +761,15 @@
         far=[1, 4, 5, 10, 11], scratch=(one_hot,),
     )
     recv = halo(faces)
-    gathered, local, *faces = call(
+    received = to_owners(message)
+    (gathered,) = call(
+        scatter_both_kernel, [gathered_shape], received, maps, scratch=lists
+    )
+    local, *faces = call(
         image_kernel,
-        [gathered_shape, vector] + halo_shapes(FACE, Far),
-        to_owners(message), maps, dof_order, weights, partial, *recv, neumann,
-        far=[2, 4, 5, 10], scratch=lists + (one_hot,),
+        [vector] + halo_shapes(FACE, Far),
+        received, dof_order, weights, partial, *recv, neumann,
+        far=[1, 3, 4, 9], scratch=(one_hot,),
     )
     recv = halo(faces)
     returned = coarse_solve(gathered, maps)

time: 196 us -> 197 us (level)
  starting transfers between devices: 58.7 us -> 72 us
  waiting for transfers between devices: 41.5 us -> 31.6 us
  blocking collectives: 51 us -> 47.9 us
    all_to_all x4, waiting for transfers between devices: 25.1 us -> 12 us  [along_z(): lax.all_to_all(value, AXES, 0, 0, axis_index_groups=column, tiled=True)]
    all_to_all x2, starting transfers between devices: 11.2 us -> 15.5 us  [to_owners(): lax.all_to_all(value, AXES, 0, 0, axis_index_groups=plane, tiled=True)]
    ppermute x4, starting transfers between devices: 15.4 us -> 19.5 us  [exchange(): other_core = lax.ppermute(other_core, 'sub', pairs(n_sub, 1))]
    ppermute x4, waiting for transfers between devices: 0.57 us -> 3.85 us  [exchange(): other_core = lax.ppermute(other_core, 'sub', pairs(n_sub, 1))]
    all_to_all x3, blocking collectives: 41.8 us -> 38.6 us  [to_owners(): lax.all_to_all(value, AXES, 0, 0, axis_index_groups=plane, tiled=True)]
    all_to_all x4, starting transfers between devices: 18.3 us -> 20.8 us  [along_z(): lax.all_to_all(value, AXES, 0, 0, axis_index_groups=column, tiled=True)]
    ppermute x4, starting transfers between devices: 7.3 us -> 9.71 us  [exchange(): slab = lax.ppermute(slab, 'grp', pairs(n_grp, 0))]
    pallas_call x12 -> x13, Pallas kernels: 40.9 us -> 41.9 us  [call(): pl.pallas_call(whole, out_shape=[pltpu.HBM(out.shape, out.dtype) if isins...]
  transfers between devices with their start and end apart: 23 -> 23, of which waited for: 8 -> 7; matrix products, arithmetic and copies ran while one was open for 0% -> 0% of each run, Pallas kernels for 5% -> 9%
where the time goes in v2:
time: 197 us; the launch traced here: 196 us
  starting transfers between devices  72 us (37%)
  blocking collectives  47.9 us (24%)
  Pallas kernels  44.4 us (23%)
  waiting for transfers between devices  31.6 us (16%)
    pallas_call x13, Pallas kernels, call(): pl.pallas_call(whole, out_shape=[pltpu.HBM(out.shape, out.dtype) if isins...  41.9 us
    all_to_all x3, blocking collectives, to_owners(): lax.all_to_all(value, AXES, 0, 0, axis_index_groups=plane, tiled=True)  38.6 us
    all_to_all x4, starting transfers between devices, along_z(): lax.all_to_all(value, AXES, 0, 0, axis_index_groups=column, tiled=True)  20.8 us
    ppermute x4, starting transfers between devices, exchange(): other_core = lax.ppermute(other_core, 'sub', pairs(n_sub, 1))  19.5 us
    all_to_all x2, starting transfers between devices, to_owners(): lax.all_to_all(value, AXES, 0, 0, axis_index_groups=plane, tiled=True)  15.5 us
    all_to_all x2, waiting for transfers between devices, to_owners(): lax.all_to_all(value, AXES, 0, 0, axis_index_groups=plane, tiled=True)  15.3 us
    all_to_all x4, waiting for transfers between devices, along_z(): lax.all_to_all(value, AXES, 0, 0, axis_index_groups=column, tiled=True)  12 us
    ppermute x4, starting transfers between devices, exchange(): slab = lax.ppermute(slab, 'grp', pairs(n_grp, 0))  9.71 us
  transfers between devices with their start and end apart: 23, of which 7 were waited for; matrix products, arithmetic and copies ran while one was open for 0% of the time, Pallas kernels for 9%

profile of v2, /device:TPU:1, one launch (start us, length us, event | category | flops | bytes accessed | tf_op | source)
XLA Modules:
  0.0 196.4 jit_solution(975959285638242311)
XLA Ops:
  0.0 3.2 %collective-permute-start.4 = (f32[128,2048]{1,0:T(8,128)}, f32[128,2048]{1,0:T(8,128)S(1)}, u32[]{:S(2)}, u32[]{:S(2)}) collective-permute-start(f32[128,2048]{1,0:T(8,128)} %own.1), channel_id=1, source_target_pairs={{0,1},{1,0},{2,3},{3,2},{4,5},{5,4},{6,7},{7,6},{8,9},{9,8},{10,11... | collective-permute-start | bytes 3145736 | tf_op jit(solution)/shard_map/ppermute | solution.py:710
  7.7 4.0 %collective-permute-start = (f32[312,128]{1,0:T(8,128)S(1)}, f32[312,128]{1,0:T(8,128)S(1)}, u32[]{:S(2)}, u32[]{:S(2)}) collective-permute-start(f32[312,128]{1,0:T(8,128)S(1)} %get-tuple-element.50), channel_id=1, source_target_pairs={{1,2},{3,4},{5,6},{7,8},{9,10},{11,12},{13,14},{2,1},{4,3},{6,5},{... | collective-permute-start | bytes 479240 | tf_op jit(solution)/shard_map/ppermute | solution.py:264
  15.5 4.7 %shard_map.84 = (f32[2,1024,128]{2,1,0:T(8,128)}, bf16[8,64,256]{2,1,0:T(8,128)(2,1)S(1)}, f32[256,128]{1,0:T(8,128)S(1)}, f32[2,256,128]{2,1,0:T(8,128)}, f32[2...) custom-call(bf16[8,256,256]{2,1,0:T(8,128)(2,1)S(1)} %get-tuple-element.48.refs_0_, ...), custom_call_target="tpu_custom_call" | custom-call | tf_op jit(solution)/shard_map/pallas_call | solution.py:168
  20.2 16.1 %all_to_all.110 = f32[32,8,128]{2,1,0:T(8,128)S(1)} all-to-all(f32[32,8,128]{2,1,0:T(8,128)S(1)} %bitcast.32), channel_id=1, replica_groups={{0,1,16,17,32,33,48,49,64,65,80,81,96,97,112,113,128,129,144,145,160,16..., dimensions={0} | all-to-all | bytes 262144 | tf_op jit(solution)/shard_map/all_to_all | solution.py:704
  38.5 8.2 %all-to-all-start.1 = ((f32[8,72,128]{2,1,0:T(8,128)}), f32[8,72,128]{2,1,0:T(8,128)S(1)}, u32[]{:S(2)}, u32[]{:S(2)}) async-start(f32[8,72,128]{2,1,0:T(8,128)} %bitcast.2), calls=%async_computation.1 | async-start | bytes 589824 | tf_op jit(solution)/shard_map/all_to_all | solution.py:707
  49.2 9.9 %all-to-all-done.1 = f32[8,72,128]{2,1,0:T(8,128)S(1)} async-done(((f32[8,72,128]{2,1,0:T(8,128)}), f32[8,72,128]{2,1,0:T(8,128)S(1)}, u32[]{:S(2)}, u32[]{:S(2)}) %all-to-all-start.1) | async-done | bytes 294944 | tf_op jit(solution)/shard_map/all_to_all | solution.py:707
  60.4 3.3 %all-to-all-start.2 = ((f32[8,8,128]{2,1,0:T(8,128)}), f32[8,8,128]{2,1,0:T(8,128)S(1)}, u32[]{:S(2)}, u32[]{:S(2)}) async-start(f32[8,8,128]{2,1,0:T(8,128)} %bitcast.4), calls=%async_computation.2 | async-start | bytes 65536 | tf_op jit(solution)/shard_map/all_to_all | solution.py:707
  63.7 4.6 %collective-permute-start.5 = (f32[256,128]{1,0:T(8,128)}, f32[256,128]{1,0:T(8,128)S(1)}, u32[]{:S(2)}, u32[]{:S(2)}) collective-permute-start(f32[256,128]{1,0:T(8,128)} %get-tuple-element.68), channel_id=1, source_target_pairs={{1,2},{3,4},{5,6},{7,8},{9,10},{11,12},{13,14},{2,1},{4,3},{6,5},{... | collective-permute-start | bytes 393224 | tf_op jit(solution)/shard_map/ppermute | solution.py:264
  72.2 5.9 %all-to-all-start.3 = ((f32[32,8,128]{2,1,0:T(8,128)}), f32[32,8,128]{2,1,0:T(8,128)S(1)}, u32[]{:S(2)}, u32[]{:S(2)}) async-start(f32[32,8,128]{2,1,0:T(8,128)} %bitcast.6), calls=%async_computation.3 | async-start | bytes 262144 | tf_op jit(solution)/shard_map/all_to_all | solution.py:704
  78.2 7.7 %all-to-all-done.3 = f32[32,8,128]{2,1,0:T(8,128)S(1)} async-done(((f32[32,8,128]{2,1,0:T(8,128)}), f32[32,8,128]{2,1,0:T(8,128)S(1)}, u32[]{:S(2)}, u32[]{:S(2)}) %all-to-all-start.3) | async-done | bytes 131104 | tf_op jit(solution)/shard_map/all_to_all | solution.py:704
  85.9 8.5 %shard_map.88 = (f32[2,1024,128]{2,1,0:T(8,128)}, f32[2,1024,128]{2,1,0:T(8,128)}, f32[256,128]{1,0:T(8,128)S(1)}, f32[2,256,128]{2,1,0:T(8,128)}, f32[2,256,128...) custom-call(f32[256,128]{1,0:T(8,128)S(1)} %bitcast.24, s32[2,4,256]{2,1,0:T(4,128)} %refs_1_.7, ...), custom_call_target="tpu_custom_call" | custom-call | tf_op jit(solution)/shard_map/pallas_call | solution.py:168
  94.4 11.3 %all_to_all.111 = f32[32,8,128]{2,1,0:T(8,128)S(1)} all-to-all(f32[32,8,128]{2,1,0:T(8,128)S(1)} %bitcast.33), channel_id=1, replica_groups={{0,1,16,17,32,33,48,49,64,65,80,81,96,97,112,113,128,129,144,145,160,16..., dimensions={0} | all-to-all | bytes 262144 | tf_op jit(solution)/shard_map/all_to_all | solution.py:704
  108.1 3.4 %all-to-all-start.5 = ((f32[8,72,128]{2,1,0:T(8,128)}), f32[8,72,128]{2,1,0:T(8,128)S(1)}, u32[]{:S(2)}, u32[]{:S(2)}) async-start(f32[8,72,128]{2,1,0:T(8,128)} %bitcast.10), calls=%async_computation.5 | async-start | bytes 589824 | tf_op jit(solution)/shard_map/all_to_all | solution.py:707
  114.0 4.4 %collective-permute-start.9 = (f32[256,128]{1,0:T(8,128)}, f32[256,128]{1,0:T(8,128)S(1)}, u32[]{:S(2)}, u32[]{:S(2)}) collective-permute-start(f32[256,128]{1,0:T(8,128)} %get-tuple-element.77), channel_id=1, source_target_pairs={{1,2},{3,4},{5,6},{7,8},{9,10},{11,12},{13,14},{2,1},{4,3},{6,5},{... | collective-permute-start | bytes 393224 | tf_op jit(solution)/shard_map/ppermute | solution.py:264
  118.5 3.3 %collective-permute-done.9.refs_5_ = f32[256,128]{1,0:T(8,128)S(1)} collective-permute-done((f32[256,128]{1,0:T(8,128)}, f32[256,128]{1,0:T(8,128)S(1)}, u32[]{:S(2)}, u32[]{:S(2)}) %collective-permute-start.9) | collective-permute-done | bytes 131104 | tf_op jit(solution)/shard_map/ppermute | solution.py:264
  121.8 7.2 %shard_map.92 = (f32[2,1024,128]{2,1,0:T(8,128)}, f32[2,256,128]{2,1,0:T(8,128)}, f32[2,256,128]{2,1,0:T(8,128)}, f32[256,128]{1,0:T(8,128)}, f32[256,128]{1,0:T(8,128)}, /*index=5*/f32[2,256,128]{2,1,0:T(8,128)}) custom-call(f32[256,128]{1,0:T(8,128)S(1)} %bitcast.23, s32[2,4,256]{2,1,0:T(4,128)} %refs_1_.7, ...), custom_call_target="tpu_custom_call" | custom-call | tf_op jit(solution)/shard_map/pallas_call | solution.py:168
  129.7 4.2 %collective-permute-start.16 = (f32[2,256,128]{2,1,0:T(8,128)}, f32[2,256,128]{2,1,0:T(8,128)S(1)}, u32[]{:S(2)}, u32[]{:S(2)}) collective-permute-start(f32[2,256,128]{2,1,0:T(8,128)} %get-tuple-element.86), channel_id=1, source_target_pairs={{0,16},{32,48},{64,80},{96,112},{128,144},{160,176},{192,208},{224... | collective-permute-start | bytes 786440 | tf_op jit(solution)/shard_map/ppermute | solution.py:266
  135.2 5.8 %all-to-all-start.6 = ((f32[8,8,128]{2,1,0:T(8,128)}), f32[8,8,128]{2,1,0:T(8,128)S(1)}, u32[]{:S(2)}, u32[]{:S(2)}) async-start(f32[8,8,128]{2,1,0:T(8,128)} %bitcast.12), calls=%async_computation.6 | async-start | bytes 65536 | tf_op jit(solution)/shard_map/all_to_all | solution.py:707
  141.0 6.5 %collective-permute-start.13 = (f32[256,128]{1,0:T(8,128)}, f32[256,128]{1,0:T(8,128)S(1)}, u32[]{:S(2)}, u32[]{:S(2)}) collective-permute-start(f32[256,128]{1,0:T(8,128)} %get-tuple-element.83), channel_id=1, source_target_pairs={{1,2},{3,4},{5,6},{7,8},{9,10},{11,12},{13,14},{2,1},{4,3},{6,5},{... | collective-permute-start | bytes 393224 | tf_op jit(solution)/shard_map/ppermute | solution.py:264
  149.6 9.6 %all-to-all-start.7 = ((f32[32,8,128]{2,1,0:T(8,128)}), f32[32,8,128]{2,1,0:T(8,128)S(1)}, u32[]{:S(2)}, u32[]{:S(2)}) async-start(f32[32,8,128]{2,1,0:T(8,128)} %bitcast.14), calls=%async_computation.7 | async-start | bytes 262144 | tf_op jit(solution)/shard_map/all_to_all | solution.py:704
  159.2 7.6 %all-to-all-done.7 = f32[32,8,128]{2,1,0:T(8,128)S(1)} async-done(((f32[32,8,128]{2,1,0:T(8,128)}), f32[32,8,128]{2,1,0:T(8,128)S(1)}, u32[]{:S(2)}, u32[]{:S(2)}) %all-to-all-start.7) | async-done | bytes 131104 | tf_op jit(solution)/shard_map/all_to_all | solution.py:704
  166.8 6.4 %shard_map.93 = (f32[2,1024,128]{2,1,0:T(8,128)}, f32[8,128]{1,0:T(8,128)S(1)}, f32[256,128]{1,0:T(8,128)S(1)}) custom-call(f32[256,128]{1,0:T(8,128)S(1)} %bitcast.25, s32[2,4,256]{2,1,0:T(4,128)} %refs_1_.7, bf16[8,64,256]{2,1,0:T(8,128)(2,1)S(1)} %get-tuple-element.65.refs_2_, f32[16,128]{1,0:T(8,128)S(1)} %get-tuple-element.54.refs_6_.refs_3_.refs_2_, ...), custom_call_target="tpu_custom_call" | custom-call | tf_op jit(solution)/shard_map/pallas_call | solution.py:168
  173.3 11.3 %all_to_all.112 = f32[32,8,128]{2,1,0:T(8,128)S(1)} all-to-all(f32[32,8,128]{2,1,0:T(8,128)S(1)} %bitcast.34), channel_id=1, replica_groups={{0,1,16,17,32,33,48,49,64,65,80,81,96,97,112,113,128,129,144,145,160,16..., dimensions={0} | all-to-all | bytes 262144 | tf_op jit(solution)/shard_map/all_to_all | solution.py:704
  184.6 9.2 %all_to_all.113 = f32[8,8,128]{2,1,0:T(8,128)S(1)} all-to-all(f32[8,8,128]{2,1,0:T(8,128)S(1)} %bitcast.31), channel_id=1, replica_groups={{0,2,4,6,8,10,12,14},{1,3,5,7,9,11,13,15},{16,18,20,22,24,26,28,30},{17..., dimensions={0} | all-to-all | bytes 65536 | tf_op jit(solution)/shard_map/all_to_all | solution.py:707
  (40 shorter events, 29.6 us)
Async XLA Ops:
  0.0 11.8 %collective-permute-start.4 = (f32[128,2048]{1,0:T(8,128)}, f32[128,2048]{1,0:T(8,128)S(1)}, u32[]{:S(2)}, u32[]{:S(2)}) collective-permute-start(f32[128,2048]{1,0:T(8,128)} %own.1), channel_id=1, source_target_pairs={{0,1},{1,0},{2,3},{3,2},{4,5},{5,4},{6,7},{7,6},{8,9},{9,8},{10,11... | collective-permute-start | bytes 3145736 | tf_op jit(solution)/shard_map/ppermute | solution.py:710
  5.1 9.9 %collective-permute-start.1 = (f32[2,312,128]{2,1,0:T(8,128)S(1)}, f32[2,312,128]{2,1,0:T(8,128)S(1)}, u32[]{:S(2)}, u32[]{:S(2)}) collective-permute-start(f32[2,312,128]{2,1,0:T(8,128)S(1)} %get-tuple-element.51), channel_id=1, source_target_pairs={{16,32},{48,64},{80,96},{112,128},{144,160},{176,192},{208,224},{3... | collective-permute-start | bytes 958472 | tf_op jit(solution)/shard_map/ppermute | solution.py:265
  5.7 9.7 %collective-permute-start.3 = (f32[2,312,128]{2,1,0:T(8,128)S(1)}, f32[2,312,128]{2,1,0:T(8,128)S(1)}, u32[]{:S(2)}, u32[]{:S(2)}) collective-permute-start(f32[2,312,128]{2,1,0:T(8,128)S(1)} %get-tuple-element.53), channel_id=1, source_target_pairs={{0,16},{32,48},{64,80},{96,112},{128,144},{160,176},{192,208},{224... | collective-permute-start | bytes 958472 | tf_op jit(solution)/shard_map/ppermute | solution.py:266
  7.7 7.2 %collective-permute-start = (f32[312,128]{1,0:T(8,128)S(1)}, f32[312,128]{1,0:T(8,128)S(1)}, u32[]{:S(2)}, u32[]{:S(2)}) collective-permute-start(f32[312,128]{1,0:T(8,128)S(1)} %get-tuple-element.50), channel_id=1, source_target_pairs={{1,2},{3,4},{5,6},{7,8},{9,10},{11,12},{13,14},{2,1},{4,3},{6,5},{... | collective-permute-start | bytes 479240 | tf_op jit(solution)/shard_map/ppermute | solution.py:264
  11.7 3.2 %collective-permute-start.2 = (f32[312,128]{1,0:T(8,128)S(1)}, f32[312,128]{1,0:T(8,128)S(1)}, u32[]{:S(2)}, u32[]{:S(2)}) collective-permute-start(f32[312,128]{1,0:T(8,128)S(1)} %get-tuple-element.52), channel_id=1, source_target_pairs={{0,1},{2,3},{4,5},{6,7},{8,9},{10,11},{12,13},{14,15},{1,0},{3,2},... | collective-permute-start | bytes 479240 | tf_op jit(solution)/shard_map/ppermute | solution.py:267
  38.5 20.5 %all-to-all-start.1 = ((f32[8,72,128]{2,1,0:T(8,128)}), f32[8,72,128]{2,1,0:T(8,128)S(1)}, u32[]{:S(2)}, u32[]{:S(2)}) async-start(f32[8,72,128]{2,1,0:T(8,128)} %bitcast.2), calls=%async_computation.1 | async-start | bytes 589824 | tf_op jit(solution)/shard_map/all_to_all | solution.py:707
  46.7 31.4 %collective-permute-start.6 = (f32[2,256,128]{2,1,0:T(8,128)}, f32[2,256,128]{2,1,0:T(8,128)S(1)}, u32[]{:S(2)}, u32[]{:S(2)}) collective-permute-start(f32[2,256,128]{2,1,0:T(8,128)} %get-tuple-element.69), channel_id=1, source_target_pairs={{16,32},{48,64},{80,96},{112,128},{144,160},{176,192},{208,224},{3... | collective-permute-start | bytes 786440 | tf_op jit(solution)/shard_map/ppermute | solution.py:265
  47.4 30.7 %collective-permute-start.8 = (f32[2,256,128]{2,1,0:T(8,128)}, f32[2,256,128]{2,1,0:T(8,128)S(1)}, u32[]{:S(2)}, u32[]{:S(2)}) collective-permute-start(f32[2,256,128]{2,1,0:T(8,128)} %get-tuple-element.71), channel_id=1, source_target_pairs={{0,16},{32,48},{64,80},{96,112},{128,144},{160,176},{192,208},{224... | collective-permute-start | bytes 786440 | tf_op jit(solution)/shard_map/ppermute | solution.py:266
  60.4 10.1 %all-to-all-start.2 = ((f32[8,8,128]{2,1,0:T(8,128)}), f32[8,8,128]{2,1,0:T(8,128)S(1)}, u32[]{:S(2)}, u32[]{:S(2)}) async-start(f32[8,8,128]{2,1,0:T(8,128)} %bitcast.4), calls=%async_computation.2 | async-start | bytes 65536 | tf_op jit(solution)/shard_map/all_to_all | solution.py:707
  63.7 14.4 %collective-permute-start.5 = (f32[256,128]{1,0:T(8,128)}, f32[256,128]{1,0:T(8,128)S(1)}, u32[]{:S(2)}, u32[]{:S(2)}) collective-permute-start(f32[256,128]{1,0:T(8,128)} %get-tuple-element.68), channel_id=1, source_target_pairs={{1,2},{3,4},{5,6},{7,8},{9,10},{11,12},{13,14},{2,1},{4,3},{6,5},{... | collective-permute-start | bytes 393224 | tf_op jit(solution)/shard_map/ppermute | solution.py:264
  68.3 9.8 %collective-permute-start.7 = (f32[256,128]{1,0:T(8,128)}, f32[256,128]{1,0:T(8,128)S(1)}, u32[]{:S(2)}, u32[]{:S(2)}) collective-permute-start(f32[256,128]{1,0:T(8,128)} %get-tuple-element.70), channel_id=1, source_target_pairs={{0,1},{2,3},{4,5},{6,7},{8,9},{10,11},{12,13},{14,15},{1,0},{3,2},... | collective-permute-start | bytes 393224 | tf_op jit(solution)/shard_map/ppermute | solution.py:267
  72.2 13.7 %all-to-all-start.3 = ((f32[32,8,128]{2,1,0:T(8,128)}), f32[32,8,128]{2,1,0:T(8,128)S(1)}, u32[]{:S(2)}, u32[]{:S(2)}) async-start(f32[32,8,128]{2,1,0:T(8,128)} %bitcast.6), calls=%async_computation.3 | async-start | bytes 262144 | tf_op jit(solution)/shard_map/all_to_all | solution.py:704
  108.1 25.8 %all-to-all-start.5 = ((f32[8,72,128]{2,1,0:T(8,128)}), f32[8,72,128]{2,1,0:T(8,128)S(1)}, u32[]{:S(2)}, u32[]{:S(2)}) async-start(f32[8,72,128]{2,1,0:T(8,128)} %bitcast.10), calls=%async_computation.5 | async-start | bytes 589824 | tf_op jit(solution)/shard_map/all_to_all | solution.py:707
  111.6 10.2 %collective-permute-start.10 = (f32[2,256,128]{2,1,0:T(8,128)}, f32[2,256,128]{2,1,0:T(8,128)S(1)}, u32[]{:S(2)}, u32[]{:S(2)}) collective-permute-start(f32[2,256,128]{2,1,0:T(8,128)} %get-tuple-element.78), channel_id=1, source_target_pairs={{16,32},{48,64},{80,96},{112,128},{144,160},{176,192},{208,224},{3... | collective-permute-start | bytes 786440 | tf_op jit(solution)/shard_map/ppermute | solution.py:265
  112.2 9.6 %collective-permute-start.12 = (f32[2,256,128]{2,1,0:T(8,128)}, f32[2,256,128]{2,1,0:T(8,128)S(1)}, u32[]{:S(2)}, u32[]{:S(2)}) collective-permute-start(f32[2,256,128]{2,1,0:T(8,128)} %get-tuple-element.80), channel_id=1, source_target_pairs={{0,16},{32,48},{64,80},{96,112},{128,144},{160,176},{192,208},{224... | collective-permute-start | bytes 786440 | tf_op jit(solution)/shard_map/ppermute | solution.py:266
  114.0 7.8 %collective-permute-start.9 = (f32[256,128]{1,0:T(8,128)}, f32[256,128]{1,0:T(8,128)S(1)}, u32[]{:S(2)}, u32[]{:S(2)}) collective-permute-start(f32[256,128]{1,0:T(8,128)} %get-tuple-element.77), channel_id=1, source_target_pairs={{1,2},{3,4},{5,6},{7,8},{9,10},{11,12},{13,14},{2,1},{4,3},{6,5},{... | collective-permute-start | bytes 393224 | tf_op jit(solution)/shard_map/ppermute | solution.py:264
  118.4 3.4 %collective-permute-start.11 = (f32[256,128]{1,0:T(8,128)}, f32[256,128]{1,0:T(8,128)S(1)}, u32[]{:S(2)}, u32[]{:S(2)}) collective-permute-start(f32[256,128]{1,0:T(8,128)} %get-tuple-element.79), channel_id=1, source_target_pairs={{0,1},{2,3},{4,5},{6,7},{8,9},{10,11},{12,13},{14,15},{1,0},{3,2},... | collective-permute-start | bytes 393224 | tf_op jit(solution)/shard_map/ppermute | solution.py:267
  129.0 30.2 %collective-permute-start.14 = (f32[2,256,128]{2,1,0:T(8,128)}, f32[2,256,128]{2,1,0:T(8,128)S(1)}, u32[]{:S(2)}, u32[]{:S(2)}) collective-permute-start(f32[2,256,128]{2,1,0:T(8,128)} %get-tuple-element.84), channel_id=1, source_target_pairs={{16,32},{48,64},{80,96},{112,128},{144,160},{176,192},{208,224},{3... | collective-permute-start | bytes 786440 | tf_op jit(solution)/shard_map/ppermute | solution.py:265
  129.7 29.5 %collective-permute-start.16 = (f32[2,256,128]{2,1,0:T(8,128)}, f32[2,256,128]{2,1,0:T(8,128)S(1)}, u32[]{:S(2)}, u32[]{:S(2)}) collective-permute-start(f32[2,256,128]{2,1,0:T(8,128)} %get-tuple-element.86), channel_id=1, source_target_pairs={{0,16},{32,48},{64,80},{96,112},{128,144},{160,176},{192,208},{224... | collective-permute-start | bytes 786440 | tf_op jit(solution)/shard_map/ppermute | solution.py:266
  135.2 12.7 %all-to-all-start.6 = ((f32[8,8,128]{2,1,0:T(8,128)}), f32[8,8,128]{2,1,0:T(8,128)S(1)}, u32[]{:S(2)}, u32[]{:S(2)}) async-start(f32[8,8,128]{2,1,0:T(8,128)} %bitcast.12), calls=%async_computation.6 | async-start | bytes 65536 | tf_op jit(solution)/shard_map/all_to_all | solution.py:707
  141.0 18.2 %collective-permute-start.13 = (f32[256,128]{1,0:T(8,128)}, f32[256,128]{1,0:T(8,128)S(1)}, u32[]{:S(2)}, u32[]{:S(2)}) collective-permute-start(f32[256,128]{1,0:T(8,128)} %get-tuple-element.83), channel_id=1, source_target_pairs={{1,2},{3,4},{5,6},{7,8},{9,10},{11,12},{13,14},{2,1},{4,3},{6,5},{... | collective-permute-start | bytes 393224 | tf_op jit(solution)/shard_map/ppermute | solution.py:264
  147.5 11.7 %collective-permute-start.15 = (f32[256,128]{1,0:T(8,128)}, f32[256,128]{1,0:T(8,128)S(1)}, u32[]{:S(2)}, u32[]{:S(2)}) collective-permute-start(f32[256,128]{1,0:T(8,128)} %get-tuple-element.85), channel_id=1, source_target_pairs={{0,1},{2,3},{4,5},{6,7},{8,9},{10,11},{12,13},{14,15},{1,0},{3,2},... | collective-permute-start | bytes 393224 | tf_op jit(solution)/shard_map/ppermute | solution.py:267
  149.6 17.2 %all-to-all-start.7 = ((f32[32,8,128]{2,1,0:T(8,128)}), f32[32,8,128]{2,1,0:T(8,128)S(1)}, u32[]{:S(2)}, u32[]{:S(2)}) async-start(f32[32,8,128]{2,1,0:T(8,128)} %bitcast.14), calls=%async_computation.7 | async-start | bytes 262144 | tf_op jit(solution)/shard_map/all_to_all | solution.py:704
